TPU v7x, 512 devices: a whole 4x4x16 slice. The times are simulated.
512 devices in a mesh: dp: 4 (over x_hi, core), seq: 128 (over x_lo, y, z).
Axes of the slice: x: 4 (x_hi: 2, x_lo: 2; x = x_hi * 2 + x_lo), y: 4, z: 16, core: 2. Of those that a mesh axis runs over, the one named last changes fastest.
Arguments:
- tokens: bfloat16 [4, 128, 512, 768], P('dp', 'seq'), may hold values from -6 to 6
- left_factor: bfloat16 [512, 512], replicated, may hold values from -0.25 to 0.25
- right_factor: bfloat16 [128, 128], replicated, may hold values from -0.5 to 0.5
- gate_kernel: float32 [128, 512], P(None, 'seq'), may hold values from 0.5 to 2
- out_grad: bfloat16 [4, 128, 512, 768], P('dp', 'seq'), may hold values from -6 to 6
Outputs:
- mixed_out: bfloat16 [4, 128, 512, 768], P('dp', 'seq')
- tokens_grad: bfloat16 [4, 128, 512, 768], P('dp', 'seq')
- left_grad: float32 [512, 512], replicated
- right_grad: float32 [128, 128], replicated
- kernel_grad: float32 [128, 512], P(None, 'seq')
All inputs are finite; a program needn't handle non-finite values.
Results may differ from a plain program's by a relative error of at most 0.0057.
Values may be sent and summed in bfloat16 or wider, within the bound.
A program may use at most 64 MiB of HBM per device.

v0:
```python
import math

import jax
import jax.numpy as jnp
from jax import lax
from jax.sharding import PartitionSpec as P


def on_device(tokens, left_factor, right_factor, gate_kernel, out_grad):
    batch_count = lax.axis_size("dp")
    width = tokens.shape[3]
    block_order = tokens.shape[2]
    first = jnp.einsum(
        "ij,bkjd->bkid", left_factor, tokens, preferred_element_type=jnp.float32
    ).astype(jnp.bfloat16)
    columns = lax.all_to_all(first, "seq", split_axis=2, concat_axis=1, tiled=True)
    block_count = columns.shape[1]
    blended = jnp.einsum("ak,bkid->baid", right_factor, columns, preferred_element_type=jnp.float32)
    gated = (gate_kernel[None, :, :, None] * blended).astype(jnp.bfloat16)
    mixed_out = lax.all_to_all(gated, "seq", split_axis=1, concat_axis=2, tiled=True)
    grad_cols = lax.all_to_all(out_grad, "seq", split_axis=2, concat_axis=1, tiled=True)
    grad_wide = grad_cols.astype(jnp.float32)
    kernel_local = jnp.sum(grad_wide * blended, axis=(0, 3)) / math.sqrt(batch_count * width)
    kernel_grad = lax.psum(kernel_local, "dp")
    weighted = (gate_kernel[None, :, :, None] * grad_wide).astype(jnp.bfloat16)
    right_local = jnp.einsum("baid,bkid->ak", weighted, columns, preferred_element_type=jnp.float32)
    right_grad = lax.psum(right_local, ("dp", "seq")) / math.sqrt(batch_count * block_order * width)
    back = jnp.einsum(
        "ak,baid->bkid", right_factor, weighted, preferred_element_type=jnp.float32
    ).astype(jnp.bfloat16)
    back_blocks = lax.all_to_all(back, "seq", split_axis=1, concat_axis=2, tiled=True)
    tokens_grad = jnp.einsum(
        "ij,bkid->bkjd", left_factor, back_blocks, preferred_element_type=jnp.float32
    ).astype(jnp.bfloat16)
    left_local = jnp.einsum(
        "bkid,bkjd->ij", back_blocks, tokens, preferred_element_type=jnp.float32
    )
    left_norm = math.sqrt(batch_count * block_count * width)
    left_total = lax.psum(left_local, ("dp", "seq"))
    left_grad = left_total / left_norm
    return (mixed_out, tokens_grad, left_grad, right_grad, kernel_grad)


def solution(mesh):
    placed = (P("dp", "seq", None, None), P(), P(), P(None, "seq"), P("dp", "seq", None, None))
    return jax.shard_map(
        on_device,
        mesh=mesh,
        in_specs=placed,
        out_specs=(
            P("dp", "seq", None, None),
            P("dp", "seq", None, None),
            P(),
            P(),
            P(None, "seq"),
        ),
        check_vma=False,
    )
```

profile of v0, /device:TPU:1, one launch (start us, length us, event | category | flops | bytes accessed | tf_op | source)
XLA Modules:
  0.0 682.8 jit_solution(14191859578316423798)
XLA Ops:
  7.2 0.0 copy-start
  7.2 2.4 copy.58
  9.6 0.5 broadcast.11
  10.1 5.4 reduce.4
  15.6 0.0 copy-start.6
  15.6 1.4 reshape.84
  16.9 22.1 %all-to-all-start.2 = ((bf16[128,2,1536]{2,1,0:T(2,128)(2,1)}), bf16[128,2,1536]{2,1,0:T(2,128)(2,1)}, u32[]{:S(2)}, u32[]{:S(2)}) async-start(bf16[128,2,1536]{2,1,0:T(2,128)(2,1)} %reshape.84), calls=%async_computation.2 | async-start | bytes 1572864 | tf_op jit(solution)/shard_map/all_to_all | solution.py:21
  39.0 0.0 copy-done
  39.0 0.6 fusion.2
  39.7 1.6 copy.34
  41.3 5.4 reduce.5
  46.7 0.0 copy-start.5
  46.7 1.4 reshape.82
  48.1 28.3 %all-to-all-done.2 = bf16[128,2,1536]{2,1,0:T(2,128)(2,1)} async-done(((bf16[128,2,1536]{2,1,0:T(2,128)(2,1)}), bf16[128,2,1536]{2,1,0:T(2,128)(2,1)}, u32[]{:S(2)}, u32[]{:S(2)}) %all-to-all-start.2) | async-done | bytes 786464 | tf_op jit(solution)/shard_map/all_to_all | solution.py:21
  76.4 14.4 %all-to-all-start = ((bf16[128,2,1536]{2,1,0:T(2,128)(2,1)}), bf16[128,2,1536]{2,1,0:T(2,128)(2,1)}, u32[]{:S(2)}, u32[]{:S(2)}) async-start(bf16[128,2,1536]{2,1,0:T(2,128)(2,1)} %reshape.82), calls=%async_computation | async-start | bytes 1572864 | tf_op jit(solution)/shard_map/all_to_all | solution.py:16
  90.8 0.1 copy.37
  90.9 5.0 reshape.85
  96.0 5.7 convert_reduce_fusion
  101.7 2.7 reshape.76
  104.4 1.8 multiply_convert_fusion
  106.2 0.0 copy-start.1
  106.2 0.9 copy-done.1
  107.1 0.4 fusion.4
  107.5 1.2 copy.40
  108.8 19.3 %all-to-all-done = bf16[128,2,1536]{2,1,0:T(2,128)(2,1)} async-done(((bf16[128,2,1536]{2,1,0:T(2,128)(2,1)}), bf16[128,2,1536]{2,1,0:T(2,128)(2,1)}, u32[]{:S(2)}, u32[]{:S(2)}) %all-to-all-start) | async-done | bytes 786464 | tf_op jit(solution)/shard_map/all_to_all | solution.py:16
  128.0 14.1 %all-to-all-start.3 = ((bf16[1,128,4,768]{3,2,0,1:T(4,128)(2,1)}), bf16[1,128,4,768]{3,2,0,1:T(4,128)(2,1)S(1)}, u32[]{:S(2)}, u32[]{:S(2)}) async-start(bf16[1,128,4,768]{3,2,0,1:T(4,128)(2,1)} %copy.40), calls=%async_computation.3 | async-start | bytes 1572864 | tf_op jit(solution)/shard_map/all_to_all | solution.py:31
  142.1 6.0 reshape.83
  148.1 6.9 %bitcast_reduce_fusion = bf16[512,768]{1,0:T(8,128)(2,1)} fusion(bf16[512,1,1,768]{3,2,1,0:T(2,128)(2,1)} %reshape.83), kind=kLoop, calls=%fused_computation.26 | loop fusion | bytes 1572864 | tf_op jit(solution)/shard_map/all_to_all | solution.py:16
  155.1 2.4 reshape.74
  157.4 3.1 copy.43
  160.5 2.1 fusion.1
  162.6 1.3 copy.36
  163.9 15.7 %all-to-all-done.3 = bf16[1,128,4,768]{3,2,0,1:T(4,128)(2,1)S(1)} async-done(((bf16[1,128,4,768]{3,2,0,1:T(4,128)(2,1)}), bf16[1,128,4,768]{3,2,0,1:T(4,128)(2,1)S(1)}, u32[]{:S(2)}, u32[]{:S(2)}) %all-to-all-start.3) | async-done | bytes 786464 | tf_op jit(solution)/shard_map/all_to_all | solution.py:31
  179.7 13.5 %all-to-all-start.1 = ((bf16[1,128,4,768]{3,2,0,1:T(4,128)(2,1)}), bf16[1,128,4,768]{3,2,0,1:T(4,128)(2,1)S(1)}, u32[]{:S(2)}, u32[]{:S(2)}) async-start(bf16[1,128,4,768]{3,2,0,1:T(4,128)(2,1)} %copy.36), calls=%async_computation.1 | async-start | bytes 1572864 | tf_op jit(solution)/shard_map/all_to_all | solution.py:20
  193.1 0.0 all-reduce.3.cloned.1.call-start
  193.2 0.0 copy-done.2
  193.2 2.1 convolution_bitcast_fusion
  195.3 0.2 reshape.75
  195.5 1.6 fusion.5
  197.1 0.0 all-reduce.3.cloned.1.call-update
  197.1 8.7 %psum.23 = f32[128,4]{0,1:T(4,128)} all-reduce(f32[128,4]{0,1:T(4,128)S(1)} %broadcast_multiply_fusion.2), channel_id=1, replica_groups=mesh['dp'=4,'seq'=128] {'dp'}, use_global_device_ids=true, to_apply=%region_3.0 | all-reduce | flops 512 | bytes 4096 | tf_op jit(solution)/shard_map/psum | solution.py:24
  205.9 1.6 fusion.3
  207.5 1.2 copy.44
  208.7 22.2 %all-to-all-done.1 = bf16[1,128,4,768]{3,2,0,1:T(4,128)(2,1)S(1)} async-done(((bf16[1,128,4,768]{3,2,0,1:T(4,128)(2,1)}), bf16[1,128,4,768]{3,2,0,1:T(4,128)(2,1)S(1)}, u32[]{:S(2)}, u32[]{:S(2)}) %all-to-all-start.1) | async-done | bytes 786464 | tf_op jit(solution)/shard_map/all_to_all | solution.py:20
  230.9 1.1 all_to_all.12
  231.9 440.6 %all-reduce.3.cloned.1.call-done = (f32[512,512]{1,0:T(8,128)}, f32[128,128]{1,0:T(8,128)}) async-done(((f32[512,512]{1,0:T(8,128)}, f32[128,128]{1,0:T(8,128)}), (f32[512,512]{1,0:T(8,128)}, f32[128,128]{1,0:T(8,128)})) %all-reduce.3.cloned.1.call-update) | async-done | bytes 1114128 | tf_op jit(solution)/shard_map/psum | solution.py:39
  672.5 2.3 broadcast_multiply_fusion
  674.9 0.6 broadcast_multiply_fusion.1
  (8 shorter events, 0.0 us)
Async XLA Ops:
  7.2 31.9 %copy-start = (bf16[1,1,512,768]{3,2,1,0:T(8,128)(2,1)S(1)}, bf16[1,1,512,768]{3,2,1,0:T(8,128)(2,1)}, u32[]{:S(2)}) copy-start(bf16[1,1,512,768]{3,2,1,0:T(8,128)(2,1)} %param.5) | copy-start | bytes 2359300
  15.6 23.5 %copy-start.6 = (bf16[512,512]{1,0:T(8,128)(2,1)S(1)}, bf16[512,512]{1,0:T(8,128)(2,1)}, u32[]{:S(2)}) copy-start(bf16[512,512]{1,0:T(8,128)(2,1)} %param.6) | copy-start | bytes 1572868
  16.9 59.5 %all-to-all-start.2 = ((bf16[128,2,1536]{2,1,0:T(2,128)(2,1)}), bf16[128,2,1536]{2,1,0:T(2,128)(2,1)}, u32[]{:S(2)}, u32[]{:S(2)}) async-start(bf16[128,2,1536]{2,1,0:T(2,128)(2,1)} %reshape.84), calls=%async_computation.2 | async-start | bytes 1572864 | tf_op jit(solution)/shard_map/all_to_all | solution.py:21
  46.7 44.1 %copy-start.5 = (f32[128,4]{0,1:T(4,128)S(1)}, f32[128,4]{0,1:T(4,128)}, u32[]{:S(2)}) copy-start(f32[128,4]{0,1:T(4,128)} %param.8) | copy-start | bytes 6148
  76.4 51.6 %all-to-all-start = ((bf16[128,2,1536]{2,1,0:T(2,128)(2,1)}), bf16[128,2,1536]{2,1,0:T(2,128)(2,1)}, u32[]{:S(2)}, u32[]{:S(2)}) async-start(bf16[128,2,1536]{2,1,0:T(2,128)(2,1)} %reshape.82), calls=%async_computation | async-start | bytes 1572864 | tf_op jit(solution)/shard_map/all_to_all | solution.py:16
  104.4 2.7 copy-start.3
  106.2 0.9 copy-start.1
  128.0 51.7 %all-to-all-start.3 = ((bf16[1,128,4,768]{3,2,0,1:T(4,128)(2,1)}), bf16[1,128,4,768]{3,2,0,1:T(4,128)(2,1)S(1)}, u32[]{:S(2)}, u32[]{:S(2)}) async-start(bf16[1,128,4,768]{3,2,0,1:T(4,128)(2,1)} %copy.40), calls=%async_computation.3 | async-start | bytes 1572864 | tf_op jit(solution)/shard_map/all_to_all | solution.py:31
  162.6 30.6 %copy-start.2 = (bf16[128,4,768]{2,1,0:T(4,128)(2,1)S(1)}, bf16[128,4,768]{2,1,0:T(4,128)(2,1)}, u32[]{:S(2)}) copy-start(bf16[128,4,768]{2,1,0:T(4,128)(2,1)} %copy-done.1) | copy-start | bytes 2359300
  179.7 51.2 %all-to-all-start.1 = ((bf16[1,128,4,768]{3,2,0,1:T(4,128)(2,1)}), bf16[1,128,4,768]{3,2,0,1:T(4,128)(2,1)S(1)}, u32[]{:S(2)}, u32[]{:S(2)}) async-start(bf16[1,128,4,768]{3,2,0,1:T(4,128)(2,1)} %copy.36), calls=%async_computation.1 | async-start | bytes 1572864 | tf_op jit(solution)/shard_map/all_to_all | solution.py:20
  193.1 479.4 %all-reduce.3.cloned.1.call-start = ((), (), s32[]{:S(2)}) async-start(), calls=%async_computation.4 | async-start | bytes 2228224 | tf_op jit(solution)/shard_map/psum | solution.py:39
  672.5 2.3 copy-start.4
Sparse Core Ops, SparseCore 0:
  200.0 472.4 all-reduce.2
where the time goes:
time: 690 us; the launch traced here: 683 us
  waiting for transfers between devices  526 us (76%)
  starting transfers between devices  64 us (9%)
  local copies, waits for them, and re-layouts  39.4 us (6%)
  other arithmetic  21.3 us (3%)
  between operations  14.7 us (2%)
  blocking collectives  8.73 us (1%)
  matrix products  8.47 us (1%)
    psum x1, waiting for transfers between devices, on_device(): left_total = lax.psum(left_local, ('dp', 'seq'))  441 us
    all_to_all x1, waiting for transfers between devices, on_device(): lax.all_to_all(out_grad, 'seq', split_axis=2, concat_axis=1, tiled=True)  28.3 us
    all_to_all x1, waiting for transfers between devices, on_device(): lax.all_to_all(gated, 'seq', split_axis=1, concat_axis=2, tiled=True)  22.2 us
    all_to_all x1, starting transfers between devices, on_device(): lax.all_to_all(out_grad, 'seq', split_axis=2, concat_axis=1, tiled=True)  22.1 us
    all_to_all x1, waiting for transfers between devices, on_device(): lax.all_to_all(first, 'seq', split_axis=2, concat_axis=1, tiled=True)  19.3 us
    unnamed x22, local copies, waits for them, and re-layouts  18.9 us
    all_to_all x1, waiting for transfers between devices, on_device(): lax.all_to_all(back, 'seq', split_axis=1, concat_axis=2, tiled=True)  15.7 us
    all_to_all x1, starting transfers between devices, on_device(): lax.all_to_all(first, 'seq', split_axis=2, concat_axis=1, tiled=True)  14.4 us
  transfers between devices with their start and end apart: 5, of which 5 were waited for; matrix products, arithmetic and copies ran while one was open for 8% of the time, Pallas kernels for 0%

commit v1 on v0

v1 whole, which is shorter than its diff:
```python
import math

import jax
import jax.numpy as jnp
from jax import lax
from jax.experimental import pallas as pl
from jax.experimental.pallas import tpu as pltpu
from jax.sharding import PartitionSpec as P

MESH = pl.DeviceIdType.MESH
BF16, F32 = jnp.bfloat16, jnp.float32
D, S2, S1, BATCH = 768, 512, 128, 4
NZ, NQ = 16, 8
ZROWS, QROWS = S2 // NZ, S2 // NQ
LANES = 256
ZORDER = [8, -7, 7, -6, 6, -5, 5, -4, 4, -3, 3, -2, 2, -1, 1]
LEFT_SCALE = 1.0 / math.sqrt(BATCH * S1 * D)
RIGHT_SCALE = 1.0 / math.sqrt(BATCH * S2 * D)
KERNEL_SCALE = 1.0 / math.sqrt(BATCH * D)


def dot(a, b, dims=((1,), (0,)), precision=None):
    return lax.dot_general(a, b, (dims, ((), ())), preferred_element_type=F32, precision=precision)


def iotas(rows, columns):
    return (
        lax.broadcasted_iota(jnp.int32, (rows, columns), 0),
        lax.broadcasted_iota(jnp.int32, (rows, columns), 1),
    )


def lane_tiles(body):
    def step(t, carry):
        body(pl.ds(pl.multiple_of(t * LANES, LANES), LANES))
        return carry

    lax.fori_loop(0, D // LANES, step, 0)


def kernel(
    tokens_hbm, left_ref, right_ref, gate_ref, grad_hbm,
    mixed_ref, tgrad_ref, lgrad_ref, rgrad_ref, kgrad_ref,
    tokens, grad_own, first, g1, g1p, g2, weighted, bo, b1, b1p, b2, f1, f1p, f2, blended, mo, m1, m1p,
    to_q, to_z, expand, mix, mix_t, gate_send, gate_mine, gate_col, ksum,
    left_local, left_mate, left_half, left_xy, right_local, right_mate, right_half, right_xy,
    z_send, z_recv, total, x_recv, piece,
    k_local, k_core, k_half, k_hi, k_total, k_home,
    load_sem, own_sem, z_ss, z_rs, q_ss, q_rs, r_ss, r_rs, rq_ss, rq_rs, rz_ss, rz_rs,
):
    dp, me = lax.axis_index("dp"), lax.axis_index("seq")
    z, q = lax.rem(me, NZ), lax.div(me, NZ)
    core, x_hi = lax.rem(dp, 2), lax.div(dp, 2)
    mate = (x_hi * 2 + (1 - core), me)
    across = ((1 - x_hi) * 2 + core, me)
    z_peers = [lax.rem(z + d + NZ, NZ) for d in ZORDER]
    q_peers = [lax.bitwise_xor(q, d) for d in range(1, NQ)]
    user = lax.rem(me, NQ) * NZ + lax.div(me, NQ)
    holder = z * NQ + q
    moves = user != me

    load_tokens = pltpu.make_async_copy(tokens_hbm, tokens, load_sem.at[0])
    load_tokens.start()
    barrier = pltpu.get_barrier_semaphore()
    for zz in z_peers:
        pl.semaphore_signal(barrier, inc=1, device_id=(dp, q * NZ + zz), device_id_type=MESH)
    for qq in q_peers:
        pl.semaphore_signal(barrier, inc=1, device_id=(dp, qq * NZ + z), device_id_type=MESH)
    pl.semaphore_signal(barrier, inc=1, device_id=mate, device_id_type=MESH)
    pl.semaphore_signal(barrier, inc=1, device_id=across, device_id_type=MESH)

    @pl.when(moves)
    def _():
        pl.semaphore_signal(barrier, inc=1, device_id=(dp, user), device_id_type=MESH)
        pl.semaphore_signal(barrier, inc=1, device_id=(dp, holder), device_id_type=MESH)

    pl.semaphore_wait(barrier, jnp.where(moves, NZ + NQ + 2, NZ + NQ))

    def send(src, dst, ss, rs, device):
        copy = pltpu.make_async_remote_copy(
            src_ref=src, dst_ref=dst, send_sem=ss, recv_sem=rs, device_id=device, device_id_type=MESH
        )
        copy.start()
        return copy

    def block(ref, index, rows):
        return ref.at[pl.ds(pl.multiple_of(index * rows, rows), rows)]

    def z_exchange(n, src, dst):
        own = pltpu.make_async_copy(block(src, z, ZROWS), block(dst, z, ZROWS), own_sem.at[n])
        own.start()
        return own, [
            send(block(src, zz, ZROWS), block(dst, z, ZROWS), z_ss.at[n, j], z_rs.at[n, j], (dp, q * NZ + zz))
            for j, zz in enumerate(z_peers)
        ]

    def q_exchange(n, src, dst):
        own = pltpu.make_async_copy(block(src, q, QROWS), block(dst, q, QROWS), own_sem.at[4 + n])
        own.start()
        return own, [
            send(block(src, qq, QROWS), block(dst, q, QROWS), q_ss.at[n, j], q_rs.at[n, j], (dp, qq * NZ + z))
            for j, qq in enumerate(q_peers)
        ]

    def arrive(exchange):
        exchange[0].wait()
        for copy in exchange[1]:
            copy.wait_recv()

    def sent(exchange):
        for copy in exchange[1]:
            copy.wait_send()

    gz = z_exchange(0, grad_hbm, g1)

    load_tokens.wait()

    def step_first(lanes):
        first[:, lanes] = dot(left_ref[...], tokens[:, lanes]).astype(BF16)

    lane_tiles(step_first)
    fz = z_exchange(1, first, f1)

    gate_send[...] = jnp.zeros((8, S1), F32)
    gate_send[0:4, :] = gate_ref[...]

    def move(src, dst, n, device):
        remote = pltpu.make_async_remote_copy(
            src_ref=src, dst_ref=dst, send_sem=r_ss.at[n], recv_sem=r_rs.at[n], device_id=device, device_id_type=MESH
        )
        local = pltpu.make_async_copy(src, dst, own_sem.at[8 + n])

        @pl.when(moves)
        def _():
            remote.start()

        @pl.when(jnp.logical_not(moves))
        def _():
            local.start()

        def finish():
            @pl.when(moves)
            def _():
                remote.wait()

            @pl.when(jnp.logical_not(moves))
            def _():
                local.wait()

        return finish

    gate_moved = move(gate_send, gate_mine, 0, (dp, user))

    r, c = iotas(S2, S2)
    to_q[...] = jnp.where((r // 4 % NZ) * ZROWS + (r // QROWS) * 4 + r % 4 == c, 1.0, 0.0).astype(BF16)
    to_z[...] = jnp.where((c // 4 % NZ) * ZROWS + (c // QROWS) * 4 + c % 4 == r, 1.0, 0.0).astype(BF16)
    re, ce = iotas(S2, S1)
    expand[...] = jnp.where(re // 4 == ce, 1.0, 0.0).astype(BF16)
    same = (r % 4 == c % 4).astype(F32)
    wide = dot(expand[...], right_ref[...]).astype(BF16)
    mix[...] = (dot(wide, expand[...], ((1,), (1,))) * same).astype(BF16)
    wide_t = dot(expand[...], right_ref[...], ((1,), (1,))).astype(BF16)
    mix_t[...] = (dot(wide_t, expand[...], ((1,), (1,))) * same).astype(BF16)
    gate_moved()
    pick = jnp.where(re % 4 == ce, 1.0, 0.0)
    gates = jnp.concatenate([gate_mine[...], jnp.zeros((S1 - 8, S1), F32)], axis=0)
    spread = dot(expand[...].astype(F32), gates, ((1,), (1,)), lax.Precision.HIGHEST)
    gate_col[...] = jnp.broadcast_to(jnp.sum(spread * pick, axis=1, keepdims=True), (S2, S1))

    def reorder(matrix, src, dst):
        def step(lanes):
            dst[:, lanes] = dot(matrix[...], src[:, lanes]).astype(BF16)

        lane_tiles(step)

    arrive(gz)
    reorder(to_q, g1, g1p)
    gq = q_exchange(0, g1p, g2)
    arrive(gq)

    def step_back(lanes):
        gate = gate_col[:, 0:1]
        w = (gate * g2[:, lanes].astype(F32)).astype(BF16)
        weighted[:, lanes] = w
        bo[:, lanes] = dot(mix_t[...], w).astype(BF16)

    lane_tiles(step_back)
    bq = q_exchange(1, bo, b1)
    arrive(bq)
    reorder(to_z, b1, b1p)
    bz = z_exchange(2, b1p, b2)

    arrive(fz)
    reorder(to_q, f1, f1p)
    fq = q_exchange(2, f1p, f2)
    arrive(fq)

    def step_mixed(lanes):
        value = dot(mix[...], f2[:, lanes])
        blended[:, lanes] = value
        mo[:, lanes] = (gate_col[:, 0:1] * value).astype(BF16)

    lane_tiles(step_mixed)
    mq = q_exchange(3, mo, m1)
    arrive(mq)
    reorder(to_z, m1, m1p)
    mz = z_exchange(3, m1p, mixed_ref)

    ksum[...] = jnp.zeros((S2, S1), F32)

    def step_kernel(lanes):
        rows = jnp.sum(g2[:, lanes].astype(F32) * blended[:, lanes], axis=1, keepdims=True)
        ksum[...] += jnp.broadcast_to(rows, (S2, S1))

    lane_tiles(step_kernel)
    by_block = dot(expand[...].astype(F32), ksum[...] * pick, ((0,), (0,)), lax.Precision.HIGHEST)
    k_local[...] = by_block.T[0:8, :]
    k1 = send(k_local, k_core, r_ss.at[1], r_rs.at[1], mate)

    left_local[...] = jnp.zeros((S2, S2), F32)

    def step_right(lanes):
        left_local[...] += dot(weighted[:, lanes], f2[:, lanes], ((1,), (1,)))

    lane_tiles(step_right)
    pairs = left_local[...] * same
    halves = dot(expand[...].astype(F32), pairs, ((0,), (0,)), lax.Precision.HIGHEST)
    right_local[...] = dot(halves, expand[...].astype(F32), ((1,), (0,)), lax.Precision.HIGHEST)

    k1.wait()
    k_half[...] = k_local[...] + k_core[...]
    k2 = send(k_half, k_hi, r_ss.at[2], r_rs.at[2], across)
    k2.wait()
    k_total[...] = (k_half[...] + k_hi[...]) * KERNEL_SCALE
    kernel_moved = move(k_total, k_home, 3, (dp, holder))

    arrive(bz)
    left_local[...] = jnp.zeros((S2, S2), F32)

    def step_left(lanes):
        left_local[...] += dot(b2[:, lanes], tokens[:, lanes], ((1,), (1,)))

    lane_tiles(step_left)

    half, quarter = S2 // 2, S1 // 2
    c1 = send(block(left_local, 1 - core, half), left_mate, r_ss.at[4], r_rs.at[4], mate)
    c2 = send(block(right_local, 1 - core, quarter), right_mate, r_ss.at[5], r_rs.at[5], mate)

    def step_tokens(lanes):
        tgrad_ref[:, lanes] = dot(left_ref[...], b2[:, lanes], ((0,), (0,))).astype(BF16)

    lane_tiles(step_tokens)
    c1.wait()
    c2.wait()
    left_half[...] = left_local[pl.ds(pl.multiple_of(core * half, half), half), :] + left_mate[...]
    right_half[...] = right_local[pl.ds(pl.multiple_of(core * quarter, quarter), quarter), :] + right_mate[...]
    rows_l, rows_r = half // NQ, quarter // NQ
    xy = []
    for j, qq in enumerate(q_peers):
        there = (dp, qq * NZ + z)
        xy.append(send(block(left_half, qq, rows_l), left_xy.at[j], rq_ss.at[0, j], rq_rs.at[0, j], there))
        xy.append(send(block(right_half, qq, rows_r), right_xy.at[j], rq_ss.at[1, j], rq_rs.at[1, j], there))
    sum_l = left_half[pl.ds(pl.multiple_of(q * rows_l, rows_l), rows_l), :]
    sum_r = right_half[pl.ds(pl.multiple_of(q * rows_r, rows_r), rows_r), :]
    for copy in xy:
        copy.wait()
    for j in range(NQ - 1):
        sum_l = sum_l + left_xy[j]
        sum_r = sum_r + right_xy[j]
    for n in range(NZ):
        z_send[n, 0:8, :] = sum_l[n // 4 * 8 : n // 4 * 8 + 8, n % 4 * 128 : n % 4 * 128 + 128]
        z_send[n, 8:16, :] = sum_r
    own_tile = pltpu.make_async_copy(z_send.at[z], z_recv.at[z], own_sem.at[12])
    own_tile.start()
    zs = [
        send(z_send.at[zz], z_recv.at[z], rz_ss.at[0, j], rz_rs.at[0, j], (dp, q * NZ + zz))
        for j, zz in enumerate(z_peers)
    ]
    own_tile.wait()
    for copy in zs:
        copy.wait()
    tiles = z_recv[0]
    for n in range(1, NZ):
        tiles = tiles + z_recv[n]
    total[...] = tiles
    xs = send(total, x_recv, r_ss.at[6], r_rs.at[6], across)
    xs.wait()
    whole = total[...] + x_recv[...]
    piece[...] = whole[0:8, :] * LEFT_SCALE
    first_row = core * half + q * rows_l
    rgrad_ref[pl.ds(pl.multiple_of(core * quarter + q * rows_r, 8), 8), :] = whole[8:16, :] * RIGHT_SCALE
    spot = lgrad_ref.at[
        pl.ds(pl.multiple_of(first_row + z // 4 * 8, 8), 8), pl.ds(pl.multiple_of(z % 4 * 128, 128), 128)
    ]
    own_piece = pltpu.make_async_copy(piece, spot, own_sem.at[13])
    own_piece.start()
    zg = [
        send(piece, spot, rz_ss.at[1, j], rz_rs.at[1, j], (dp, q * NZ + zz)) for j, zz in enumerate(z_peers)
    ]
    own_piece.wait()
    for copy in zg:
        copy.wait()
    part_l = lgrad_ref.at[pl.ds(pl.multiple_of(first_row, rows_l), rows_l)]
    part_r = rgrad_ref.at[pl.ds(pl.multiple_of(core * quarter + q * rows_r, rows_r), rows_r)]
    xg = []
    for j, qq in enumerate(q_peers):
        there = (dp, qq * NZ + z)
        xg.append(send(part_l, part_l, rq_ss.at[2, j], rq_rs.at[2, j], there))
        xg.append(send(part_r, part_r, rq_ss.at[3, j], rq_rs.at[3, j], there))
    for copy in xg:
        copy.wait()
    half_l, half_r = block(lgrad_ref, core, half), block(rgrad_ref, core, quarter)
    h1 = send(half_l, half_l, r_ss.at[7], r_rs.at[7], mate)
    h2 = send(half_r, half_r, r_ss.at[8], r_rs.at[8], mate)
    kernel_moved()
    kgrad_ref[...] = k_home[0:4, :]
    h1.wait()
    h2.wait()

    arrive(mz)
    for exchange in (gz, fz, gq, bq, bz, fq, mq, mz):
        sent(exchange)


def on_device(tokens, left_factor, right_factor, gate_kernel, out_grad):
    vmem = pl.BlockSpec(memory_space=pltpu.VMEM)
    hbm = pl.BlockSpec(memory_space=pl.ANY)
    plane = pltpu.VMEM((S2, D), BF16)
    square = pltpu.VMEM((S2, S2), BF16)
    tile = pltpu.VMEM((8, S1), F32)
    half, quarter = S2 // 2, S1 // 2
    dma = pltpu.SemaphoreType.DMA
    mixed, tgrad, lgrad, rgrad, kgrad = pl.pallas_call(
        kernel,
        name="monarch",
        out_shape=(
            jax.ShapeDtypeStruct((S2, D), BF16),
            jax.ShapeDtypeStruct((S2, D), BF16),
            jax.ShapeDtypeStruct((S2, S2), F32),
            jax.ShapeDtypeStruct((S1, S1), F32),
            jax.ShapeDtypeStruct((4, S1), F32),
        ),
        in_specs=[hbm, vmem, vmem, vmem, hbm],
        out_specs=(vmem,) * 5,
        scratch_shapes=[
            *[plane] * 14,
            pltpu.VMEM((S2, D), F32),
            *[plane] * 3,
            square, square, pltpu.VMEM((S2, S1), BF16), square, square,
            tile, tile, pltpu.VMEM((S2, S1), F32), pltpu.VMEM((S2, S1), F32),
            pltpu.VMEM((S2, S2), F32), pltpu.VMEM((half, S2), F32), pltpu.VMEM((half, S2), F32),
            pltpu.VMEM((NQ - 1, half // NQ, S2), F32),
            pltpu.VMEM((S1, S1), F32), pltpu.VMEM((quarter, S1), F32), pltpu.VMEM((quarter, S1), F32),
            pltpu.VMEM((NQ - 1, quarter // NQ, S1), F32),
            pltpu.VMEM((NZ, 16, S1), F32), pltpu.VMEM((NZ, 16, S1), F32),
            pltpu.VMEM((16, S1), F32), pltpu.VMEM((16, S1), F32), tile,
            *[tile] * 6,
            dma((1,)), dma((14,)), dma((4, NZ - 1)), dma((4, NZ - 1)), dma((4, NQ - 1)), dma((4, NQ - 1)),
            dma((9,)), dma((9,)), dma((4, NQ - 1)), dma((4, NQ - 1)), dma((2, NZ - 1)), dma((2, NZ - 1)),
        ],
        compiler_params=pltpu.CompilerParams(
            collective_id=0, has_side_effects=True, vmem_limit_bytes=56 * 1024 * 1024
        ),
    )(tokens.reshape(S2, D), left_factor, right_factor, gate_kernel.T, out_grad.reshape(S2, D))
    return mixed.reshape(tokens.shape), tgrad.reshape(tokens.shape), lgrad, rgrad, kgrad.T


def solution(mesh):
    blocks = P("dp", "seq", None, None)
    return jax.shard_map(
        on_device,
        mesh=mesh,
        in_specs=(blocks, P(), P(), P(None, "seq"), blocks),
        out_specs=(blocks, blocks, P(), P(), P(None, "seq")),
        check_vma=False,
    )
```

time: 690 us -> 223 us (0.32)
  waiting for transfers between devices: 526 us -> 0 us
  Pallas kernels: 0 us -> 216 us
  starting transfers between devices: 64 us -> 0 us
  local copies, waits for them, and re-layouts: 39.4 us -> 5.88 us
  other arithmetic: 21.3 us -> 0 us
  between operations: 14.7 us -> 0.65 us
  blocking collectives: 8.73 us -> 0 us
  matrix products: 8.47 us -> 0 us
    psum x1 -> x0, waiting for transfers between devices: 441 us -> none  [on_device(): left_total = lax.psum(left_local, ('dp', 'seq'))]
    pallas_call x0 -> x1, Pallas kernels: none -> 216 us  [on_device(): pl.pallas_call(kernel, name='monarch', out_shape=(jax.ShapeDtypeStruct((S...]
    all_to_all x4 -> x0, waiting for transfers between devices: 85.6 us -> none  [the longest x1 28.3 us: on_device(): lax.all_to_all(out_grad, 'seq', split_axis=2, concat_axis=1, tiled=True)]
    all_to_all x4 -> x0, starting transfers between devices: 64 us -> none  [the longest x1 22.1 us: on_device(): lax.all_to_all(out_grad, 'seq', split_axis=2, concat_axis=1, tiled=True)]
    unnamed x22 -> x13, local copies, waits for them, and re-layouts: 18.9 us -> 5.88 us
    unnamed x2 -> x0, other arithmetic: 10.9 us -> none
    convert_element_type x5 -> x0, local copies, waits for them, and re-layouts: 9.93 us -> none  [the longest x2 5.79 us: on_device(): grad_wide = grad_cols.astype(jnp.float32)]
    psum x1 -> x0, blocking collectives: 8.73 us -> none  [on_device(): kernel_grad = lax.psum(kernel_local, 'dp')]
  transfers between devices with their start and end apart: 5 -> 0, of which waited for: 5 -> 0; matrix products, arithmetic and copies ran while one was open for 8% -> 0% of each run, Pallas kernels for 0% -> 0%
where the time goes in v1:
time: 223 us
  Pallas kernels  216 us (97%)
  local copies, waits for them, and re-layouts  5.88 us (3%)
    pallas_call x1, Pallas kernels, on_device(): pl.pallas_call(kernel, name='monarch', out_shape=(jax.ShapeDtypeStruct((S...  216 us
    unnamed x13, local copies, waits for them, and re-layouts  5.88 us

profile of v1, /device:TPU:1, one launch (start us, length us, event | category | flops | bytes accessed | tf_op | source)
XLA Modules:
  0.0 222.6 jit_solution(3898159174609517543)
XLA Ops:
  0.6 216.1 %monarch.1 = (bf16[512,768]{1,0:T(8,128)(2,1)}, bf16[512,768]{1,0:T(8,128)(2,1)}, f32[512,512]{1,0:T(8,128)}, f32[128,128]{1,0:T(8,128)}, f32[4,128]{1,0:T(4,128)}) custom-call(bf16[512,768]{1,0:T(8,128)(2,1)} %bitcast.6, bf16[512,512]{1,0:T(8,128)(2,1)} %left_ref.1, bf16[128,128]{1,0:T(8,128)(2,1)} %right_ref.1, f32[4,128]{1,0:T(4,128)} %bitcast.10, ...), custom_call_target="tpu_custom_call" | custom-call | tf_op jit(solution)/shard_map/monarch/pallas_call | solution.py:333
  216.8 0.0 copy-start.1
  216.8 2.1 copy.15
  218.9 0.0 copy-done.1
  218.9 0.0 copy-start
  218.9 0.9 copy.16
  219.8 0.6 copy-done
  220.4 0.0 copy-start.2
  220.4 1.0 copy.17
  221.4 0.0 copy-done.2
  221.4 0.0 copy-start.3
  221.4 0.6 copy.18
  222.0 0.0 copy-done.3
  222.1 0.6 copy.19
Async XLA Ops:
  216.8 2.1 copy-start.1
  218.9 1.5 copy-start
  220.4 1.0 copy-start.2
  221.4 0.7 copy-start.3

commit v2 on v1

v2 whole, which is shorter than its diff:
```python
import math

import jax
import jax.numpy as jnp
from jax import lax
from jax.experimental import pallas as pl
from jax.experimental.pallas import tpu as pltpu
from jax.sharding import PartitionSpec as P

MESH = pl.DeviceIdType.MESH
BF16, F32 = jnp.bfloat16, jnp.float32
D, S2, S1, BATCH = 768, 512, 128, 4
NZ, NQ, NC = 16, 8, 16
ZROWS, QROWS = S2 // NZ, S2 // NQ
LANES = 256
ZORDER = [8, -7, 7, -6, 6, -5, 5, -4, 4, -3, 3, -2, 2, -1, 1]
MPARTS = [[8, -7, 7], [-6, 6], [-5, 5, -4, 4, -3, 3, -2, 2, -1, 1]]
KEEP_PARTS = 4
VMEM_LIMIT = 56 * 1024 * 1024
LEFT_SCALE = 1.0 / math.sqrt(BATCH * S1 * D)
RIGHT_SCALE = 1.0 / math.sqrt(BATCH * S2 * D)
KERNEL_SCALE = 1.0 / math.sqrt(BATCH * D)


def dot(a, b, dims=((1,), (0,)), precision=None):
    return lax.dot_general(a, b, (dims, ((), ())), preferred_element_type=F32, precision=precision)


def iotas(rows, columns):
    return (
        lax.broadcasted_iota(jnp.int32, (rows, columns), 0),
        lax.broadcasted_iota(jnp.int32, (rows, columns), 1),
    )


def lane_tiles(body):
    def step(t, carry):
        body(pl.ds(pl.multiple_of(t * LANES, LANES), LANES))
        return carry

    lax.fori_loop(0, D // LANES, step, 0)


def kernel(
    tokens_hbm, left_hbm, right_hbm, gate_hbm, grad_hbm,
    mixed_ref, tgrad_ref, lgrad_ref, rgrad_ref, kgrad_ref,
    tokens, left_ref, right_ref, first, g1, g1p, g2, weighted, bo, b1, b1p, b2, f1, f1p, f2, blended, mo, m1, m1p, tgrad,
    to_q, to_z, expand, mix, mix_t, gate_mine, gate_col, ksum,
    left_give, left_mate, left_half, left_xy, z_send, z_recv, piece,
    lgrad, pairs, right_local, right_xy, right_sum, right_mate, right_half, right_z, right_piece, rgrad,
    k_local, k_core, k_half, k_hi, k_total, k_home,
    load_sem, own_sem, z_ss, z_rs, q_ss, q_rs, s_ss, s_rs, x_ss, x_rs,
):
    dp, me = lax.axis_index("dp"), lax.axis_index("seq")
    z, q = lax.rem(me, NZ), lax.div(me, NZ)
    core, x_hi = lax.rem(dp, 2), lax.div(dp, 2)
    chip = x_hi * NQ + q
    mate = (x_hi * 2 + (1 - core), me)
    across = ((1 - x_hi) * 2 + core, me)
    z_peers = [lax.rem(z + d + NZ, NZ) for d in ZORDER]
    q_peers = [lax.bitwise_xor(q, d) for d in range(1, NQ)]
    chip_peers = [lax.bitwise_xor(chip, d) for d in range(1, NC)]

    def along_z(zz):
        return (dp, q * NZ + zz)

    def along_q(qq):
        return (dp, qq * NZ + z)

    def at_chip(cc):
        return (lax.div(cc, NQ) * 2 + core, lax.rem(cc, NQ) * NZ + z)

    user = lax.rem(me, NQ) * NZ + lax.div(me, NQ)
    holder = z * NQ + q
    moves = user != me

    barrier = pltpu.get_barrier_semaphore()

    def greet(device):
        pl.semaphore_signal(barrier, inc=1, device_id=device, device_id_type=MESH)

    for zz in z_peers:
        greet(along_z(zz))

    @pl.when(moves)
    def _():
        greet((dp, user))
        greet((dp, holder))

    for cc in chip_peers:
        greet(at_chip(cc))
    greet(mate)
    loads = [
        pltpu.make_async_copy(src, dst, load_sem.at[n])
        for n, (src, dst) in enumerate([(tokens_hbm, tokens), (left_hbm, left_ref), (right_hbm, right_ref)])
    ]
    for load in loads:
        load.start()
    pl.semaphore_wait(barrier, jnp.where(moves, NZ + NC + 1, NZ + NC - 1))

    def send(src, dst, ss, rs, device):
        copy = pltpu.make_async_remote_copy(
            src_ref=src, dst_ref=dst, send_sem=ss, recv_sem=rs, device_id=device, device_id_type=MESH
        )
        copy.start()
        return copy

    def block(ref, index, rows):
        return ref.at[pl.ds(pl.multiple_of(index * rows, rows), rows)]

    def z_part(n, src, dst, distances):
        for d in distances:
            zz = z_peers[ZORDER.index(d)]
            send(block(src, zz, ZROWS), block(dst, z, ZROWS), z_ss.at[n], z_rs.at[n], along_z(zz))

    def z_own(n, src, dst):
        own = pltpu.make_async_copy(block(src, z, ZROWS), block(dst, z, ZROWS), own_sem.at[n])
        own.start()
        return own

    def q_exchange(n, src, dst):
        own = pltpu.make_async_copy(block(src, q, QROWS), block(dst, q, QROWS), own_sem.at[4 + n])
        own.start()
        for qq in q_peers:
            send(block(src, qq, QROWS), block(dst, q, QROWS), q_ss.at[n], q_rs.at[n], along_q(qq))
        return own

    def bytes_of(ref, sem):
        pltpu.make_async_copy(ref, ref, sem).wait()

    def z_bytes(ref, sem):
        bytes_of(ref.at[pl.ds(0, S2 - ZROWS)], sem)

    def q_bytes(ref, sem):
        bytes_of(ref.at[pl.ds(0, S2 - QROWS)], sem)

    def z_arrive(n, own, dst):
        own.wait()
        z_bytes(dst, z_rs.at[n])

    def q_arrive(n, own, dst):
        own.wait()
        q_bytes(dst, q_rs.at[n])

    def move(src, dst, n, device):
        remote = pltpu.make_async_remote_copy(
            src_ref=src, dst_ref=dst, send_sem=s_ss.at[n], recv_sem=s_rs.at[n], device_id=device, device_id_type=MESH
        )
        local = pltpu.make_async_copy(src, dst, own_sem.at[8 + n])

        @pl.when(moves)
        def _():
            remote.start()

        @pl.when(jnp.logical_not(moves))
        def _():
            local.start()

        def finish():
            @pl.when(moves)
            def _():
                remote.wait()

            @pl.when(jnp.logical_not(moves))
            def _():
                local.wait()

        return finish

    gate_moved = move(gate_hbm, gate_mine, 0, (dp, user))
    z_part(0, grad_hbm, g1, ZORDER)
    g_own = z_own(0, grad_hbm, g1)

    loads[0].wait()
    loads[1].wait()

    def step_first(lanes):
        first[:, lanes] = dot(left_ref[...], tokens[:, lanes]).astype(BF16)

    lane_tiles(step_first)

    r, c = iotas(S2, S2)
    to_q[...] = jnp.where((r // 4 % NZ) * ZROWS + (r // QROWS) * 4 + r % 4 == c, 1.0, 0.0).astype(BF16)
    to_z[...] = jnp.where((c // 4 % NZ) * ZROWS + (c // QROWS) * 4 + c % 4 == r, 1.0, 0.0).astype(BF16)
    re, ce = iotas(S2, S1)
    expand[...] = jnp.where(re // 4 == ce, 1.0, 0.0).astype(BF16)
    same = (r % 4 == c % 4).astype(F32)
    loads[2].wait()
    wide = dot(expand[...], right_ref[...]).astype(BF16)
    mix[...] = (dot(wide, expand[...], ((1,), (1,))) * same).astype(BF16)
    wide_t = dot(expand[...], right_ref[...], ((1,), (1,))).astype(BF16)
    mix_t[...] = (dot(wide_t, expand[...], ((1,), (1,))) * same).astype(BF16)
    gate_moved()
    pick = jnp.where(re % 4 == ce, 1.0, 0.0)
    gates = jnp.concatenate([gate_mine[...], jnp.zeros((S1 - 4, S1), F32)], axis=0)
    z_bytes(g1, z_ss.at[0])
    f_own = z_own(1, first, f1)
    z_part(1, first, f1, ZORDER)
    spread = dot(expand[...].astype(F32), gates, ((1,), (1,)), lax.Precision.HIGHEST)
    gate_col[...] = jnp.broadcast_to(jnp.sum(spread * pick, axis=1, keepdims=True), (S2, S1))

    def reorder(matrix, src, dst):
        def step(lanes):
            dst[:, lanes] = dot(matrix[...], src[:, lanes]).astype(BF16)

        lane_tiles(step)

    z_arrive(0, g_own, g1)
    reorder(to_q, g1, g1p)
    q_arrive(0, q_exchange(0, g1p, g2), g2)

    def step_back(lanes):
        w = (gate_col[:, 0:1] * g2[:, lanes].astype(F32)).astype(BF16)
        weighted[:, lanes] = w
        bo[:, lanes] = dot(mix_t[...], w).astype(BF16)

    lane_tiles(step_back)
    q_arrive(1, q_exchange(1, bo, b1), b1)
    reorder(to_z, b1, b1p)
    z_part(2, b1p, b2, ZORDER)
    b_own = z_own(2, b1p, b2)

    z_arrive(1, f_own, f1)
    reorder(to_q, f1, f1p)
    q_arrive(2, q_exchange(2, f1p, f2), f2)

    def step_mixed(lanes):
        value = dot(mix[...], f2[:, lanes])
        blended[:, lanes] = value
        mo[:, lanes] = (gate_col[:, 0:1] * value).astype(BF16)

    lane_tiles(step_mixed)
    mq_own = q_exchange(3, mo, m1)

    ksum[...] = jnp.zeros((S2, S1), F32)

    def step_kernel(lanes):
        rows = jnp.sum(g2[:, lanes].astype(F32) * blended[:, lanes], axis=1, keepdims=True)
        ksum[...] += jnp.broadcast_to(rows, (S2, S1))

    lane_tiles(step_kernel)
    by_block = dot(expand[...].astype(F32), ksum[...] * pick, ((0,), (0,)), lax.Precision.HIGHEST)
    k_local[...] = by_block.T[0:4, :]
    k1 = send(k_local, k_core, s_ss.at[1], s_rs.at[1], mate)

    pairs[...] = jnp.zeros((S2, S2), F32)

    def step_right(lanes):
        pairs[...] += dot(weighted[:, lanes], f2[:, lanes], ((1,), (1,)))

    lane_tiles(step_right)
    halves = dot(expand[...].astype(F32), pairs[...] * same, ((0,), (0,)), lax.Precision.HIGHEST)
    right_local[...] = dot(halves, expand[...].astype(F32), ((1,), (0,)), lax.Precision.HIGHEST)
    for j, cc in enumerate(chip_peers):
        send(block(right_local, cc, 8), right_xy.at[j], s_ss.at[6], s_rs.at[6], at_chip(cc))
    k1.wait()
    k_half[...] = k_local[...] + k_core[...]
    k2 = send(k_half, k_hi, s_ss.at[2], s_rs.at[2], across)

    q_arrive(3, mq_own, m1)
    reorder(to_z, m1, m1p)
    k2.wait()
    k_total[...] = (k_half[...] + k_hi[...]) * KERNEL_SCALE
    kernel_moved = move(k_total, k_home, 3, (dp, holder))
    sum_r = right_local[pl.ds(pl.multiple_of(chip * 8, 8), 8), :]
    bytes_of(right_xy, s_ss.at[6])
    bytes_of(right_xy, s_rs.at[6])
    for j in range(NC - 1):
        sum_r = sum_r + right_xy[j]
    right_sum[...] = sum_r
    rm = send(right_sum, right_mate, s_ss.at[4], s_rs.at[4], mate)
    m_own = z_own(3, m1p, mixed_ref)
    rm.wait()
    right_half[...] = right_sum[...] + right_mate[...]
    right_z[z] = right_half[...]
    for zz in z_peers:
        send(right_half, right_z.at[z], s_ss.at[7], s_rs.at[7], along_z(zz))
    z_bytes(b2, z_ss.at[2])
    z_part(3, m1p, mixed_ref, MPARTS[0])

    z_arrive(2, b_own, b2)
    half = S2 // 2
    rows_l = half // NC

    def left_rows(index):
        rows = b2[pl.ds(pl.multiple_of(index * half, half), half), :]
        return dot(rows, tokens[...], ((1,), (1,)))

    left_give[...] = left_rows(1 - core)
    c1 = send(left_give, left_mate, s_ss.at[5], s_rs.at[5], mate)
    left_half[...] = left_rows(core)
    c1.wait()
    left_half[...] += left_mate[...]
    for j, cc in enumerate(chip_peers):
        send(block(left_half, cc, rows_l), left_xy.at[j], s_ss.at[8], s_rs.at[8], at_chip(cc))

    def step_tokens(lanes):
        tgrad[:, lanes] = dot(left_ref[...], b2[:, lanes], ((0,), (0,))).astype(BF16)

    lane_tiles(step_tokens)
    save_tokens = pltpu.make_async_copy(tgrad, tgrad_ref, own_sem.at[12])
    save_tokens.start()

    sum_l = left_half[pl.ds(pl.multiple_of(chip * rows_l, rows_l), rows_l), :]
    bytes_of(left_xy, s_ss.at[8])
    bytes_of(left_xy, s_rs.at[8])
    for j in range(NC - 1):
        sum_l = sum_l + left_xy[j]
    for n in range(8):
        z_send[n] = sum_l[n // 4 * 8 : n // 4 * 8 + 8, n % 4 * 128 : n % 4 * 128 + 128]
    z_recv[z] = z_send[lax.rem(z, 8)]
    for zz in z_peers:
        send(z_send.at[lax.rem(zz, 8)], z_recv.at[z], s_ss.at[9], s_rs.at[9], along_z(zz))
    z_part(3, m1p, mixed_ref, MPARTS[1])

    z_tiles = right_z.at[pl.ds(0, NZ - 1)]
    bytes_of(z_tiles, s_ss.at[7])
    bytes_of(z_tiles, s_rs.at[7])
    whole_r = right_z[0]
    for n in range(1, NZ):
        whole_r = whole_r + right_z[n]
    right_piece[...] = whole_r * RIGHT_SCALE
    rgrad[pl.ds(pl.multiple_of(chip * 8, 8), 8), :] = right_piece[...]
    for cc in chip_peers:
        send(right_piece, block(rgrad, chip, 8), s_ss.at[10], s_rs.at[10], at_chip(cc))

    bytes_of(z_tiles, s_ss.at[9])
    bytes_of(z_tiles, s_rs.at[9])
    whole_l = z_recv[0]
    for n in range(1, NZ):
        whole_l = whole_l + z_recv[n]
    piece[...] = whole_l * LEFT_SCALE
    first_row = core * half + chip * rows_l
    part = lax.rem(z, 8)
    spot_l = lgrad.at[
        pl.ds(pl.multiple_of(first_row + part // 4 * 8, 8), 8), pl.ds(pl.multiple_of(part % 4 * 128, 128), 128)
    ]
    own_l = pltpu.make_async_copy(piece, spot_l, own_sem.at[13])
    own_l.start()
    for d in (-4, 3, -3, 2, -2, 1, -1):
        zz = z_peers[ZORDER.index(d)]
        send(piece, spot_l, s_ss.at[11], s_rs.at[11], along_z(zz))
    z_part(3, m1p, mixed_ref, MPARTS[2])
    own_l.wait()
    seven = z_recv.at[pl.ds(0, 7)]
    bytes_of(seven, s_ss.at[11])
    bytes_of(seven, s_rs.at[11])

    def part_l(which, cc):
        return lgrad.at[pl.ds(pl.multiple_of(which * half + cc * rows_l, rows_l), rows_l)]

    mine = part_l(core, chip)
    lx = [send(mine, mine, x_ss.at[0], x_rs.at[j], at_chip(cc)) for j, cc in enumerate(chip_peers)]
    send(mine, mine, x_ss.at[1], s_rs.at[12], mate)
    for j, cc in enumerate(chip_peers):
        lx[j].wait_recv()
        send(part_l(core, cc), part_l(core, cc), x_ss.at[1], s_rs.at[12], mate)
    kernel_moved()
    bytes_of(right_xy, s_ss.at[10])
    bytes_of(right_xy, s_rs.at[10])
    saves = [
        pltpu.make_async_copy(src, dst, own_sem.at[14 + n])
        for n, (src, dst) in enumerate([(k_home, kgrad_ref), (rgrad, rgrad_ref), (lgrad, lgrad_ref)])
    ]
    saves[0].start()
    saves[1].start()
    bytes_of(left_xy, x_ss.at[0])
    bytes_of(lgrad.at[pl.ds(0, half)], x_ss.at[1])
    bytes_of(lgrad.at[pl.ds(0, half)], s_rs.at[12])
    saves[2].start()
    save_tokens.wait()
    z_bytes(f1, z_ss.at[1])
    z_bytes(m1p, z_ss.at[3])
    for n, buffer in enumerate([g2, b1, f2, m1]):
        q_bytes(buffer, q_ss.at[n])
    z_arrive(3, m_own, m1p)
    for save in saves:
        save.wait()


def keep(*refs):
    pieces = []
    for n in range(5):
        rows = refs[n].shape[0]
        step = max(rows // KEEP_PARTS, 4) if rows == S2 else rows
        pieces += [(n, at, step) for at in range(0, rows, step)]
    load_sem, save_sem = refs[15], refs[16]
    loads, saves = [], []
    for i, (n, at, step) in enumerate(pieces):
        spot = pl.ds(at, step)
        loads.append(pltpu.make_async_copy(refs[n].at[spot], refs[10 + n].at[spot], load_sem.at[i]))
        saves.append(pltpu.make_async_copy(refs[10 + n].at[spot], refs[5 + n].at[spot], save_sem.at[i]))
        loads[-1].start()
    for load, save in zip(loads, saves):
        load.wait()
        save.start()
    for save in saves:
        save.wait()


def on_device(tokens, left_factor, right_factor, gate_kernel, out_grad):
    hbm = pl.BlockSpec(memory_space=pl.ANY)
    plane = pltpu.VMEM((S2, D), BF16)
    square = pltpu.VMEM((S2, S2), BF16)
    tile, four = pltpu.VMEM((8, S1), F32), pltpu.VMEM((4, S1), F32)
    half = S2 // 2
    dma = pltpu.SemaphoreType.DMA
    results = (
        jax.ShapeDtypeStruct((S2, D), BF16),
        jax.ShapeDtypeStruct((S2, D), BF16),
        jax.ShapeDtypeStruct((S2, S2), F32),
        jax.ShapeDtypeStruct((S1, S1), F32),
        jax.ShapeDtypeStruct((4, S1), F32),
    )
    made = pl.pallas_call(
        kernel,
        name="monarch",
        out_shape=results,
        in_specs=[hbm] * 5,
        out_specs=(hbm,) * 5,
        scratch_shapes=[
            plane, square, pltpu.VMEM((S1, S1), BF16),
            *[plane] * 12,
            pltpu.VMEM((S2, D), F32),
            *[plane] * 4,
            square, square, pltpu.VMEM((S2, S1), BF16), square, square,
            four, pltpu.VMEM((S2, S1), F32), pltpu.VMEM((S2, S1), F32),
            *[pltpu.VMEM((half, S2), F32)] * 3,
            pltpu.VMEM((NC - 1, half // NC, S2), F32),
            pltpu.VMEM((8, 8, S1), F32), pltpu.VMEM((NZ, 8, S1), F32), tile,
            pltpu.VMEM((S2, S2), F32), pltpu.VMEM((S2, S2), F32), pltpu.VMEM((S1, S1), F32),
            pltpu.VMEM((NC - 1, 8, S1), F32), tile, tile, tile, pltpu.VMEM((NZ, 8, S1), F32), tile,
            pltpu.VMEM((S1, S1), F32),
            *[four] * 6,
            dma((3,)), dma((17,)), dma((4,)), dma((4,)), dma((4,)), dma((4,)),
            dma((13,)), dma((13,)), dma((2,)), dma((NC - 1,)),
        ],
        compiler_params=pltpu.CompilerParams(
            collective_id=0, has_side_effects=True, vmem_limit_bytes=VMEM_LIMIT
        ),
    )(tokens.reshape(S2, D), left_factor, right_factor, gate_kernel.T, out_grad.reshape(S2, D))
    mixed, tgrad, lgrad, rgrad, kgrad = pl.pallas_call(
        keep,
        name="keep",
        out_shape=results,
        in_specs=[hbm] * 5,
        out_specs=(hbm,) * 5,
        scratch_shapes=[
            *[pltpu.VMEM(result.shape, result.dtype) for result in results],
            dma((3 * KEEP_PARTS + 2,)), dma((3 * KEEP_PARTS + 2,)),
        ],
    )(*made)
    return mixed.reshape(tokens.shape), tgrad.reshape(tokens.shape), lgrad, rgrad, kgrad.T


def solution(mesh):
    blocks = P("dp", "seq", None, None)
    return jax.shard_map(
        on_device,
        mesh=mesh,
        in_specs=(blocks, P(), P(), P(None, "seq"), blocks),
        out_specs=(blocks, blocks, P(), P(), P(None, "seq")),
        check_vma=False,
    )
```

time: 223 us -> 168 us (0.75)
  Pallas kernels: 216 us -> 166 us
  local copies, waits for them, and re-layouts: 5.88 us -> 0 us
    pallas_call x1 -> x2, Pallas kernels: 216 us -> 166 us  [the longest x1 163 us: on_device(): pl.pallas_call(kernel, name='monarch', out_shape=results, in_specs=[hbm]...]
    unnamed x13 -> x0, local copies, waits for them, and re-layouts: 5.88 us -> none
where the time goes in v2:
time: 168 us; the launch traced here: 167 us
  Pallas kernels  166 us (99%)
    pallas_call x1, Pallas kernels, on_device(): pl.pallas_call(kernel, name='monarch', out_shape=results, in_specs=[hbm]...  163 us

profile of v2, /device:TPU:1, one launch (start us, length us, event | category | flops | bytes accessed | tf_op | source)
XLA Modules:
  0.0 166.8 jit_solution(10369111008848730337)
XLA Ops:
  0.6 163.4 %monarch.1 = (bf16[512,768]{1,0:T(8,128)(2,1)}, bf16[512,768]{1,0:T(8,128)(2,1)}, f32[512,512]{1,0:T(8,128)}, f32[128,128]{1,0:T(8,128)}, f32[4,128]{1,0:T(4,128)}) custom-call(bf16[512,768]{1,0:T(8,128)(2,1)} %bitcast.6, bf16[512,512]{1,0:T(8,128)(2,1)} %left_hbm.1, bf16[128,128]{1,0:T(8,128)(2,1)} %right_hbm.1, f32[4,128]{1,0:T(4,128)} %bitcast.8, ...), custom_call_target="tpu_custom_call" | custom-call | tf_op jit(solution)/shard_map/monarch/pallas_call | solution.py:415
  164.0 2.8 %keep.1 = (bf16[512,768]{1,0:T(8,128)(2,1)}, bf16[512,768]{1,0:T(8,128)(2,1)}, f32[512,512]{1,0:T(8,128)}, f32[128,128]{1,0:T(8,128)}, f32[4,128]{1,0:T(4,128)}) custom-call(bf16[512,768]{1,0:T(8,128)(2,1)} %get-tuple-element.15.refs_0_, bf16[512,768]{1,0:T(8,128)(2,1)} %get-tuple-element.16.refs_1_, f32[512,512]{1,0:T(8,128)} %get-tuple-element.17.refs_2_, ...), custom_call_target="tpu_custom_call" | custom-call | tf_op jit(solution)/shard_map/keep/pallas_call | solution.py:442

commit v3 on v2

--- a/solution.py
+++ b/solution.py
@@ -14,7 +14,9 @@
 ZROWS, QROWS = S2 // NZ, S2 // NQ
 LANES = 256
 ZORDER = [8, -7, 7, -6, 6, -5, 5, -4, 4, -3, 3, -2, 2, -1, 1]
-MPARTS = [[8, -7, 7], [-6, 6], [-5, 5, -4, 4, -3, 3, -2, 2, -1, 1]]
+MPARTS = [[8, -7, 7, -1, 1], [-6, 6, -4, 4, -3, 3], [-5, 5, -2, 2]]
+LASTPARTS = [[8, -7, 7], [-6, 6, -5, 5, -4, 4, -3, 3, -2, 2, -1, 1]]
+LPARTS = [(0, 512), (512, 256)]
 KEEP_PARTS = 4
 VMEM_LIMIT = 56 * 1024 * 1024
 LEFT_SCALE = 1.0 / math.sqrt(BATCH * S1 * D)
@@ -33,12 +35,12 @@
     )
 
 
-def lane_tiles(body):
+def lane_tiles(body, part=(0, D)):
     def step(t, carry):
         body(pl.ds(pl.multiple_of(t * LANES, LANES), LANES))
         return carry
 
-    lax.fori_loop(0, D // LANES, step, 0)
+    lax.fori_loop(part[0] // LANES, (part[0] + part[1]) // LANES, step, 0)
 
 
 def kernel(
@@ -105,48 +107,59 @@
         copy.start()
         return copy
 
-    def block(ref, index, rows):
-        return ref.at[pl.ds(pl.multiple_of(index * rows, rows), rows)]
-
-    def z_part(n, src, dst, distances):
+    def block(ref, index, rows, lanes=None):
+        spot = pl.ds(pl.multiple_of(index * rows, rows), rows)
+        return ref.at[spot] if lanes is None else ref.at[spot, pl.ds(*lanes)]
+
+    def z_part(n, p, src, dst, distances):
         for d in distances:
             zz = z_peers[ZORDER.index(d)]
-            send(block(src, zz, ZROWS), block(dst, z, ZROWS), z_ss.at[n], z_rs.at[n], along_z(zz))
-
-    def z_own(n, src, dst):
-        own = pltpu.make_async_copy(block(src, z, ZROWS), block(dst, z, ZROWS), own_sem.at[n])
+            send(
+                block(src, zz, ZROWS, LPARTS[p]), block(dst, z, ZROWS, LPARTS[p]),
+                z_ss.at[2 * n + p], z_rs.at[2 * n + p], along_z(zz),
+            )
+
+    def z_own(n, p, src, dst):
+        own = pltpu.make_async_copy(
+            block(src, z, ZROWS, LPARTS[p]), block(dst, z, ZROWS, LPARTS[p]), own_sem.at[2 * n + p]
+        )
         own.start()
         return own
 
-    def q_exchange(n, src, dst):
-        own = pltpu.make_async_copy(block(src, q, QROWS), block(dst, q, QROWS), own_sem.at[4 + n])
+    def q_exchange(n, p, src, dst):
+        own = pltpu.make_async_copy(
+            block(src, q, QROWS, LPARTS[p]), block(dst, q, QROWS, LPARTS[p]), own_sem.at[8 + 2 * n + p]
+        )
         own.start()
         for qq in q_peers:
-            send(block(src, qq, QROWS), block(dst, q, QROWS), q_ss.at[n], q_rs.at[n], along_q(qq))
+            send(
+                block(src, qq, QROWS, LPARTS[p]), block(dst, q, QROWS, LPARTS[p]),
+                q_ss.at[2 * n + p], q_rs.at[2 * n + p], along_q(qq),
+            )
         return own
 
     def bytes_of(ref, sem):
         pltpu.make_async_copy(ref, ref, sem).wait()
 
-    def z_bytes(ref, sem):
-        bytes_of(ref.at[pl.ds(0, S2 - ZROWS)], sem)
-
-    def q_bytes(ref, sem):
-        bytes_of(ref.at[pl.ds(0, S2 - QROWS)], sem)
-
-    def z_arrive(n, own, dst):
+    def z_bytes(p, ref, sem):
+        bytes_of(ref.at[pl.ds(0, S2 - ZROWS), pl.ds(*LPARTS[p])], sem)
+
+    def q_bytes(p, ref, sem):
+        bytes_of(ref.at[pl.ds(0, S2 - QROWS), pl.ds(*LPARTS[p])], sem)
+
+    def z_arrive(n, p, own, dst):
         own.wait()
-        z_bytes(dst, z_rs.at[n])
-
-    def q_arrive(n, own, dst):
+        z_bytes(p, dst, z_rs.at[2 * n + p])
+
+    def q_arrive(n, p, own, dst):
         own.wait()
-        q_bytes(dst, q_rs.at[n])
+        q_bytes(p, dst, q_rs.at[2 * n + p])
 
     def move(src, dst, n, device):
         remote = pltpu.make_async_remote_copy(
             src_ref=src, dst_ref=dst, send_sem=s_ss.at[n], recv_sem=s_rs.at[n], device_id=device, device_id_type=MESH
         )
-        local = pltpu.make_async_copy(src, dst, own_sem.at[8 + n])
+        local = pltpu.make_async_copy(src, dst, own_sem.at[16 + n])
 
         @pl.when(moves)
         def _():
@@ -168,8 +181,9 @@
         return finish
 
     gate_moved = move(gate_hbm, gate_mine, 0, (dp, user))
-    z_part(0, grad_hbm, g1, ZORDER)
-    g_own = z_own(0, grad_hbm, g1)
+    z_part(0, 0, grad_hbm, g1, ZORDER)
+    z_part(0, 1, grad_hbm, g1, ZORDER)
+    g_own = [z_own(0, p, grad_hbm, g1) for p in (0, 1)]
 
     loads[0].wait()
     loads[1].wait()
@@ -193,102 +207,86 @@
     gate_moved()
     pick = jnp.where(re % 4 == ce, 1.0, 0.0)
     gates = jnp.concatenate([gate_mine[...], jnp.zeros((S1 - 4, S1), F32)], axis=0)
-    z_bytes(g1, z_ss.at[0])
-    f_own = z_own(1, first, f1)
-    z_part(1, first, f1, ZORDER)
     spread = dot(expand[...].astype(F32), gates, ((1,), (1,)), lax.Precision.HIGHEST)
     gate_col[...] = jnp.broadcast_to(jnp.sum(spread * pick, axis=1, keepdims=True), (S2, S1))
 
-    def reorder(matrix, src, dst):
+    def reorder(matrix, p, src, dst):
         def step(lanes):
             dst[:, lanes] = dot(matrix[...], src[:, lanes]).astype(BF16)
 
-        lane_tiles(step)
-
-    z_arrive(0, g_own, g1)
-    reorder(to_q, g1, g1p)
-    q_arrive(0, q_exchange(0, g1p, g2), g2)
+        lane_tiles(step, LPARTS[p])
 
     def step_back(lanes):
         w = (gate_col[:, 0:1] * g2[:, lanes].astype(F32)).astype(BF16)
         weighted[:, lanes] = w
         bo[:, lanes] = dot(mix_t[...], w).astype(BF16)
 
-    lane_tiles(step_back)
-    q_arrive(1, q_exchange(1, bo, b1), b1)
-    reorder(to_z, b1, b1p)
-    z_part(2, b1p, b2, ZORDER)
-    b_own = z_own(2, b1p, b2)
-
-    z_arrive(1, f_own, f1)
-    reorder(to_q, f1, f1p)
-    q_arrive(2, q_exchange(2, f1p, f2), f2)
-
     def step_mixed(lanes):
         value = dot(mix[...], f2[:, lanes])
         blended[:, lanes] = value
         mo[:, lanes] = (gate_col[:, 0:1] * value).astype(BF16)
 
-    lane_tiles(step_mixed)
-    mq_own = q_exchange(3, mo, m1)
-
     ksum[...] = jnp.zeros((S2, S1), F32)
+    pairs[...] = jnp.zeros((S2, S2), F32)
 
     def step_kernel(lanes):
         rows = jnp.sum(g2[:, lanes].astype(F32) * blended[:, lanes], axis=1, keepdims=True)
         ksum[...] += jnp.broadcast_to(rows, (S2, S1))
 
-    lane_tiles(step_kernel)
-    by_block = dot(expand[...].astype(F32), ksum[...] * pick, ((0,), (0,)), lax.Precision.HIGHEST)
-    k_local[...] = by_block.T[0:4, :]
-    k1 = send(k_local, k_core, s_ss.at[1], s_rs.at[1], mate)
-
-    pairs[...] = jnp.zeros((S2, S2), F32)
-
     def step_right(lanes):
         pairs[...] += dot(weighted[:, lanes], f2[:, lanes], ((1,), (1,)))
 
-    lane_tiles(step_right)
-    halves = dot(expand[...].astype(F32), pairs[...] * same, ((0,), (0,)), lax.Precision.HIGHEST)
-    right_local[...] = dot(halves, expand[...].astype(F32), ((1,), (0,)), lax.Precision.HIGHEST)
-    for j, cc in enumerate(chip_peers):
-        send(block(right_local, cc, 8), right_xy.at[j], s_ss.at[6], s_rs.at[6], at_chip(cc))
-    k1.wait()
-    k_half[...] = k_local[...] + k_core[...]
-    k2 = send(k_half, k_hi, s_ss.at[2], s_rs.at[2], across)
-
-    q_arrive(3, mq_own, m1)
-    reorder(to_z, m1, m1p)
-    k2.wait()
-    k_total[...] = (k_half[...] + k_hi[...]) * KERNEL_SCALE
-    kernel_moved = move(k_total, k_home, 3, (dp, holder))
-    sum_r = right_local[pl.ds(pl.multiple_of(chip * 8, 8), 8), :]
-    bytes_of(right_xy, s_ss.at[6])
-    bytes_of(right_xy, s_rs.at[6])
-    for j in range(NC - 1):
-        sum_r = sum_r + right_xy[j]
-    right_sum[...] = sum_r
-    rm = send(right_sum, right_mate, s_ss.at[4], s_rs.at[4], mate)
-    m_own = z_own(3, m1p, mixed_ref)
-    rm.wait()
-    right_half[...] = right_sum[...] + right_mate[...]
-    right_z[z] = right_half[...]
-    for zz in z_peers:
-        send(right_half, right_z.at[z], s_ss.at[7], s_rs.at[7], along_z(zz))
-    z_bytes(b2, z_ss.at[2])
-    z_part(3, m1p, mixed_ref, MPARTS[0])
-
-    z_arrive(2, b_own, b2)
+    z_bytes(0, g1, z_ss.at[0])
+    f_own = [z_own(1, p, first, f1) for p in (0, 1)]
+    z_part(1, 0, first, f1, ZORDER)
+
+    z_arrive(0, 0, g_own[0], g1)
+    reorder(to_q, 0, g1, g1p)
+    q_arrive(0, 0, q_exchange(0, 0, g1p, g2), g2)
+    lane_tiles(step_back, LPARTS[0])
+    bq0 = q_exchange(1, 0, bo, b1)
+    z_arrive(0, 1, g_own[1], g1)
+    reorder(to_q, 1, g1, g1p)
+    gq1 = q_exchange(0, 1, g1p, g2)
+    q_arrive(1, 0, bq0, b1)
+    reorder(to_z, 0, b1, b1p)
+    z_part(2, 0, b1p, b2, ZORDER)
+    q_arrive(0, 1, gq1, g2)
+    lane_tiles(step_back, LPARTS[1])
+    q_arrive(1, 1, q_exchange(1, 1, bo, b1), b1)
+    reorder(to_z, 1, b1, b1p)
+    z_part(2, 1, b1p, b2, ZORDER)
+    b_own = [z_own(2, p, b1p, b2) for p in (0, 1)]
+
+    z_arrive(1, 0, f_own[0], f1)
+    reorder(to_q, 0, f1, f1p)
+    q_arrive(2, 0, q_exchange(2, 0, f1p, f2), f2)
+    lane_tiles(step_mixed, LPARTS[0])
+    mq0 = q_exchange(3, 0, mo, m1)
+    lane_tiles(step_kernel, LPARTS[0])
+    lane_tiles(step_right, LPARTS[0])
+    q_arrive(3, 0, mq0, m1)
+    reorder(to_z, 0, m1, m1p)
+    z_bytes(0, b2, z_ss.at[4])
+    z_part(1, 1, first, f1, ZORDER)
+
     half = S2 // 2
     rows_l = half // NC
 
-    def left_rows(index):
-        rows = b2[pl.ds(pl.multiple_of(index * half, half), half), :]
-        return dot(rows, tokens[...], ((1,), (1,)))
-
-    left_give[...] = left_rows(1 - core)
+    def left_rows(index, p):
+        spot = pl.ds(pl.multiple_of(index * half, half), half)
+        lanes = pl.ds(*LPARTS[p])
+        return dot(b2[spot, lanes], tokens[:, lanes], ((1,), (1,)))
+
+    z_arrive(2, 0, b_own[0], b2)
+    left_give[...] = left_rows(1 - core, 0)
+    left_half[...] = left_rows(core, 0)
+    m_own = [z_own(3, 0, m1p, mixed_ref)]
+    z_arrive(2, 1, b_own[1], b2)
+    left_give[...] += left_rows(1 - core, 1)
     c1 = send(left_give, left_mate, s_ss.at[5], s_rs.at[5], mate)
-    left_half[...] = left_rows(core)
+    z_part(3, 0, m1p, mixed_ref, MPARTS[0])
+    left_half[...] += left_rows(core, 1)
     c1.wait()
     left_half[...] += left_mate[...]
     for j, cc in enumerate(chip_peers):
@@ -298,8 +296,12 @@
         tgrad[:, lanes] = dot(left_ref[...], b2[:, lanes], ((0,), (0,))).astype(BF16)
 
     lane_tiles(step_tokens)
-    save_tokens = pltpu.make_async_copy(tgrad, tgrad_ref, own_sem.at[12])
+    save_tokens = pltpu.make_async_copy(tgrad, tgrad_ref, own_sem.at[20])
     save_tokens.start()
+
+    z_arrive(1, 1, f_own[1], f1)
+    reorder(to_q, 1, f1, f1p)
+    fq1 = q_exchange(2, 1, f1p, f2)
 
     sum_l = left_half[pl.ds(pl.multiple_of(chip * rows_l, rows_l), rows_l), :]
     bytes_of(left_xy, s_ss.at[8])
@@ -311,19 +313,27 @@
     z_recv[z] = z_send[lax.rem(z, 8)]
     for zz in z_peers:
         send(z_send.at[lax.rem(zz, 8)], z_recv.at[z], s_ss.at[9], s_rs.at[9], along_z(zz))
-    z_part(3, m1p, mixed_ref, MPARTS[1])
+    z_part(3, 0, m1p, mixed_ref, MPARTS[1])
+
+    q_arrive(2, 1, fq1, f2)
+    lane_tiles(step_mixed, LPARTS[1])
+    mq1 = q_exchange(3, 1, mo, m1)
+
+    lane_tiles(step_kernel, LPARTS[1])
+    by_block = dot(expand[...].astype(F32), ksum[...] * pick, ((0,), (0,)), lax.Precision.HIGHEST)
+    k_local[...] = by_block.T[0:4, :]
+    k1 = send(k_local, k_core, s_ss.at[1], s_rs.at[1], mate)
+
+    lane_tiles(step_right, LPARTS[1])
+    halves = dot(expand[...].astype(F32), pairs[...] * same, ((0,), (0,)), lax.Precision.HIGHEST)
+    right_local[...] = dot(halves, expand[...].astype(F32), ((1,), (0,)), lax.Precision.HIGHEST)
+    for j, cc in enumerate(chip_peers):
+        send(block(right_local, cc, 8), right_xy.at[j], s_ss.at[6], s_rs.at[6], at_chip(cc))
+    k1.wait()
+    k_half[...] = k_local[...] + k_core[...]
+    k2 = send(k_half, k_hi, s_ss.at[2], s_rs.at[2], across)
 
     z_tiles = right_z.at[pl.ds(0, NZ - 1)]
-    bytes_of(z_tiles, s_ss.at[7])
-    bytes_of(z_tiles, s_rs.at[7])
-    whole_r = right_z[0]
-    for n in range(1, NZ):
-        whole_r = whole_r + right_z[n]
-    right_piece[...] = whole_r * RIGHT_SCALE
-    rgrad[pl.ds(pl.multiple_of(chip * 8, 8), 8), :] = right_piece[...]
-    for cc in chip_peers:
-        send(right_piece, block(rgrad, chip, 8), s_ss.at[10], s_rs.at[10], at_chip(cc))
-
     bytes_of(z_tiles, s_ss.at[9])
     bytes_of(z_tiles, s_rs.at[9])
     whole_l = z_recv[0]
@@ -335,12 +345,31 @@
     spot_l = lgrad.at[
         pl.ds(pl.multiple_of(first_row + part // 4 * 8, 8), 8), pl.ds(pl.multiple_of(part % 4 * 128, 128), 128)
     ]
-    own_l = pltpu.make_async_copy(piece, spot_l, own_sem.at[13])
+    own_l = pltpu.make_async_copy(piece, spot_l, own_sem.at[21])
     own_l.start()
     for d in (-4, 3, -3, 2, -2, 1, -1):
         zz = z_peers[ZORDER.index(d)]
         send(piece, spot_l, s_ss.at[11], s_rs.at[11], along_z(zz))
-    z_part(3, m1p, mixed_ref, MPARTS[2])
+    sum_r = right_local[pl.ds(pl.multiple_of(chip * 8, 8), 8), :]
+    bytes_of(right_xy, s_ss.at[6])
+    bytes_of(right_xy, s_rs.at[6])
+    for j in range(NC - 1):
+        sum_r = sum_r + right_xy[j]
+    right_half[...] = sum_r
+    right_z[z] = sum_r
+    for zz in z_peers:
+        send(right_half, right_z.at[z], s_ss.at[7], s_rs.at[7], along_z(zz))
+    z_part(3, 0, m1p, mixed_ref, MPARTS[2])
+
+    q_arrive(3, 1, mq1, m1)
+    reorder(to_z, 1, m1, m1p)
+    m_own.append(z_own(3, 1, m1p, mixed_ref))
+    z_part(3, 1, m1p, mixed_ref, LASTPARTS[0])
+    k2.wait()
+    k_total[...] = (k_half[...] + k_hi[...]) * KERNEL_SCALE
+    kernel_moved = move(k_total, k_home, 3, (dp, holder))
+    z_part(3, 1, m1p, mixed_ref, LASTPARTS[1])
+
     own_l.wait()
     seven = z_recv.at[pl.ds(0, 7)]
     bytes_of(seven, s_ss.at[11])
@@ -352,28 +381,46 @@
     mine = part_l(core, chip)
     lx = [send(mine, mine, x_ss.at[0], x_rs.at[j], at_chip(cc)) for j, cc in enumerate(chip_peers)]
     send(mine, mine, x_ss.at[1], s_rs.at[12], mate)
+
+    bytes_of(z_tiles, s_ss.at[7])
+    bytes_of(z_tiles, s_rs.at[7])
+    whole_r = right_z[0]
+    for n in range(1, NZ):
+        whole_r = whole_r + right_z[n]
+    right_sum[...] = whole_r
+    rm = send(right_sum, right_mate, s_ss.at[4], s_rs.at[4], mate)
+    rm.wait()
+    right_piece[...] = (right_sum[...] + right_mate[...]) * RIGHT_SCALE
+    rgrad[pl.ds(pl.multiple_of(chip * 8, 8), 8), :] = right_piece[...]
+    for cc in chip_peers:
+        send(right_piece, block(rgrad, chip, 8), s_ss.at[10], s_rs.at[10], at_chip(cc))
     for j, cc in enumerate(chip_peers):
         lx[j].wait_recv()
         send(part_l(core, cc), part_l(core, cc), x_ss.at[1], s_rs.at[12], mate)
+    bytes_of(left_xy, x_ss.at[0])
+    bytes_of(lgrad.at[pl.ds(0, half)], x_ss.at[1])
+    bytes_of(lgrad.at[pl.ds(0, half)], s_rs.at[12])
+    save_left = pltpu.make_async_copy(lgrad, lgrad_ref, own_sem.at[24])
+    save_left.start()
     kernel_moved()
     bytes_of(right_xy, s_ss.at[10])
     bytes_of(right_xy, s_rs.at[10])
     saves = [
-        pltpu.make_async_copy(src, dst, own_sem.at[14 + n])
-        for n, (src, dst) in enumerate([(k_home, kgrad_ref), (rgrad, rgrad_ref), (lgrad, lgrad_ref)])
+        pltpu.make_async_copy(src, dst, own_sem.at[22 + n])
+        for n, (src, dst) in enumerate([(k_home, kgrad_ref), (rgrad, rgrad_ref)])
     ]
-    saves[0].start()
-    saves[1].start()
-    bytes_of(left_xy, x_ss.at[0])
-    bytes_of(lgrad.at[pl.ds(0, half)], x_ss.at[1])
-    bytes_of(lgrad.at[pl.ds(0, half)], s_rs.at[12])
-    saves[2].start()
+    for save in saves:
+        save.start()
     save_tokens.wait()
-    z_bytes(f1, z_ss.at[1])
-    z_bytes(m1p, z_ss.at[3])
+    save_left.wait()
+    for n, p, buffer in [(0, 1, g1), (1, 0, f1), (1, 1, f1), (2, 1, b2), (3, 0, m1p), (3, 1, m1p)]:
+        z_bytes(p, buffer, z_ss.at[2 * n + p])
     for n, buffer in enumerate([g2, b1, f2, m1]):
-        q_bytes(buffer, q_ss.at[n])
-    z_arrive(3, m_own, m1p)
+        for p in (0, 1):
+            q_bytes(p, buffer, q_ss.at[2 * n + p])
+    for p in (0, 1):
+        m_own[p].wait()
+        z_bytes(p, m1p, z_rs.at[6 + p])
     for save in saves:
         save.wait()
 
@@ -432,7 +479,7 @@
             pltpu.VMEM((NC - 1, 8, S1), F32), tile, tile, tile, pltpu.VMEM((NZ, 8, S1), F32), tile,
             pltpu.VMEM((S1, S1), F32),
             *[four] * 6,
-            dma((3,)), dma((17,)), dma((4,)), dma((4,)), dma((4,)), dma((4,)),
+            dma((3,)), dma((25,)), dma((8,)), dma((8,)), dma((8,)), dma((8,)),
             dma((13,)), dma((13,)), dma((2,)), dma((NC - 1,)),
         ],
         compiler_params=pltpu.CompilerParams(

time: 168 us -> 164 us (0.976)
  Pallas kernels: 166 us -> 164 us
    pallas_call x1, Pallas kernels: 163 us -> 161 us  [on_device(): pl.pallas_call(kernel, name='monarch', out_shape=results, in_specs=[hbm]...]
where the time goes in v3:
time: 164 us
  Pallas kernels  164 us (100%)
    pallas_call x1, Pallas kernels, on_device(): pl.pallas_call(kernel, name='monarch', out_shape=results, in_specs=[hbm]...  161 us

profile of v3, /device:TPU:1, one launch (start us, length us, event | category | flops | bytes accessed | tf_op | source)
XLA Modules:
  0.0 164.3 jit_solution(3558446343721540135)
XLA Ops:
  0.6 160.9 %monarch.1 = (bf16[512,768]{1,0:T(8,128)(2,1)}, bf16[512,768]{1,0:T(8,128)(2,1)}, f32[512,512]{1,0:T(8,128)}, f32[128,128]{1,0:T(8,128)}, f32[4,128]{1,0:T(4,128)}) custom-call(bf16[512,768]{1,0:T(8,128)(2,1)} %bitcast.6, bf16[512,512]{1,0:T(8,128)(2,1)} %left_hbm.1, bf16[128,128]{1,0:T(8,128)(2,1)} %right_hbm.1, f32[4,128]{1,0:T(4,128)} %bitcast.8, ...), custom_call_target="tpu_custom_call" | custom-call | tf_op jit(solution)/shard_map/monarch/pallas_call | solution.py:462
  161.5 2.8 %keep.1 = (bf16[512,768]{1,0:T(8,128)(2,1)}, bf16[512,768]{1,0:T(8,128)(2,1)}, f32[512,512]{1,0:T(8,128)}, f32[128,128]{1,0:T(8,128)}, f32[4,128]{1,0:T(4,128)}) custom-call(bf16[512,768]{1,0:T(8,128)(2,1)} %get-tuple-element.15.refs_0_, bf16[512,768]{1,0:T(8,128)(2,1)} %get-tuple-element.16.refs_1_, f32[512,512]{1,0:T(8,128)} %get-tuple-element.17.refs_2_, ...), custom_call_target="tpu_custom_call" | custom-call | tf_op jit(solution)/shard_map/keep/pallas_call | solution.py:489

commit v4 on v3

--- a/solution.py
+++ b/solution.py
@@ -46,10 +46,10 @@
 def kernel(
     tokens_hbm, left_hbm, right_hbm, gate_hbm, grad_hbm,
     mixed_ref, tgrad_ref, lgrad_ref, rgrad_ref, kgrad_ref,
-    tokens, left_ref, right_ref, first, g1, g1p, g2, weighted, bo, b1, b1p, b2, f1, f1p, f2, blended, mo, m1, m1p, tgrad,
+    grad, tokens, left_ref, right_ref, first, g1, g1p, g2, weighted, bo, b1, b1p, b2, f1, f1p, f2, blended, mo, m1, m1p, tgrad,
     to_q, to_z, expand, mix, mix_t, gate_mine, gate_col, ksum,
-    left_give, left_mate, left_half, left_xy, z_send, z_recv, piece,
-    lgrad, pairs, right_local, right_xy, right_sum, right_mate, right_half, right_z, right_piece, rgrad,
+    left_give, left_mate, left_half, left_xy, z_send, z_recv, piece, z_gather, own_rows,
+    lgrad, pairs, right_local, right_xy, right_half, right_z, right_piece, right_all, rgrad,
     k_local, k_core, k_half, k_hi, k_total, k_home,
     load_sem, own_sem, z_ss, z_rs, q_ss, q_rs, s_ss, s_rs, x_ss, x_rs,
 ):
@@ -69,13 +69,27 @@
     def along_q(qq):
         return (dp, qq * NZ + z)
 
-    def at_chip(cc):
-        return (lax.div(cc, NQ) * 2 + core, lax.rem(cc, NQ) * NZ + z)
+    def at_chip(cc, on=core):
+        return (lax.div(cc, NQ) * 2 + on, lax.rem(cc, NQ) * NZ + z)
+
+    plane_peers = [(at_chip(cc), core * NC + cc) for cc in chip_peers]
+    for d in range(NC):
+        cc = lax.bitwise_xor(chip, d)
+        plane_peers.append((at_chip(cc, 1 - core), (1 - core) * NC + cc))
+    number = core * NC + chip
 
     user = lax.rem(me, NQ) * NZ + lax.div(me, NQ)
     holder = z * NQ + q
     moves = user != me
 
+    loads = [
+        pltpu.make_async_copy(src, dst, load_sem.at[n])
+        for n, (src, dst) in enumerate(
+            [(grad_hbm, grad), (tokens_hbm, tokens), (left_hbm, left_ref), (right_hbm, right_ref)]
+        )
+    ]
+    for load in loads:
+        load.start()
     barrier = pltpu.get_barrier_semaphore()
 
     def greet(device):
@@ -91,14 +105,9 @@
 
     for cc in chip_peers:
         greet(at_chip(cc))
-    greet(mate)
-    loads = [
-        pltpu.make_async_copy(src, dst, load_sem.at[n])
-        for n, (src, dst) in enumerate([(tokens_hbm, tokens), (left_hbm, left_ref), (right_hbm, right_ref)])
-    ]
-    for load in loads:
-        load.start()
-    pl.semaphore_wait(barrier, jnp.where(moves, NZ + NC + 1, NZ + NC - 1))
+    for d in range(NC):
+        greet(at_chip(lax.bitwise_xor(chip, d), 1 - core))
+    pl.semaphore_wait(barrier, jnp.where(moves, NZ + 2 * NC, NZ + 2 * NC - 2))
 
     def send(src, dst, ss, rs, device):
         copy = pltpu.make_async_remote_copy(
@@ -181,12 +190,13 @@
         return finish
 
     gate_moved = move(gate_hbm, gate_mine, 0, (dp, user))
-    z_part(0, 0, grad_hbm, g1, ZORDER)
-    z_part(0, 1, grad_hbm, g1, ZORDER)
-    g_own = [z_own(0, p, grad_hbm, g1) for p in (0, 1)]
-
     loads[0].wait()
+    z_part(0, 0, grad, g1, ZORDER)
+    z_part(0, 1, grad, g1, ZORDER)
+    g_own = [z_own(0, p, grad, g1) for p in (0, 1)]
+
     loads[1].wait()
+    loads[2].wait()
 
     def step_first(lanes):
         first[:, lanes] = dot(left_ref[...], tokens[:, lanes]).astype(BF16)
@@ -199,7 +209,7 @@
     re, ce = iotas(S2, S1)
     expand[...] = jnp.where(re // 4 == ce, 1.0, 0.0).astype(BF16)
     same = (r % 4 == c % 4).astype(F32)
-    loads[2].wait()
+    loads[3].wait()
     wide = dot(expand[...], right_ref[...]).astype(BF16)
     mix[...] = (dot(wide, expand[...], ((1,), (1,))) * same).astype(BF16)
     wide_t = dot(expand[...], right_ref[...], ((1,), (1,))).astype(BF16)
@@ -308,11 +318,11 @@
     bytes_of(left_xy, s_rs.at[8])
     for j in range(NC - 1):
         sum_l = sum_l + left_xy[j]
-    for n in range(8):
-        z_send[n] = sum_l[n // 4 * 8 : n // 4 * 8 + 8, n % 4 * 128 : n % 4 * 128 + 128]
-    z_recv[z] = z_send[lax.rem(z, 8)]
+    for n in range(NZ):
+        z_send[n] = sum_l[n // 4 * 4 : n // 4 * 4 + 4, n % 4 * 128 : n % 4 * 128 + 128]
+    z_recv[z] = z_send[z]
     for zz in z_peers:
-        send(z_send.at[lax.rem(zz, 8)], z_recv.at[z], s_ss.at[9], s_rs.at[9], along_z(zz))
+        send(z_send.at[zz], z_recv.at[z], s_ss.at[9], s_rs.at[9], along_z(zz))
     z_part(3, 0, m1p, mixed_ref, MPARTS[1])
 
     q_arrive(2, 1, fq1, f2)
@@ -326,13 +336,11 @@
 
     lane_tiles(step_right, LPARTS[1])
     halves = dot(expand[...].astype(F32), pairs[...] * same, ((0,), (0,)), lax.Precision.HIGHEST)
-    right_local[...] = dot(halves, expand[...].astype(F32), ((1,), (0,)), lax.Precision.HIGHEST)
-    for j, cc in enumerate(chip_peers):
-        send(block(right_local, cc, 8), right_xy.at[j], s_ss.at[6], s_rs.at[6], at_chip(cc))
-    k1.wait()
-    k_half[...] = k_local[...] + k_core[...]
-    k2 = send(k_half, k_hi, s_ss.at[2], s_rs.at[2], across)
-
+    rights = dot(halves, expand[...].astype(F32), ((1,), (0,)), lax.Precision.HIGHEST)
+    for n in range(2 * NC):
+        right_local[n] = rights[4 * n : 4 * n + 4, :]
+    for j, (there, n) in enumerate(plane_peers):
+        send(right_local.at[n], right_xy.at[j], s_ss.at[6], s_rs.at[6], there)
     z_tiles = right_z.at[pl.ds(0, NZ - 1)]
     bytes_of(z_tiles, s_ss.at[9])
     bytes_of(z_tiles, s_rs.at[9])
@@ -340,26 +348,24 @@
     for n in range(1, NZ):
         whole_l = whole_l + z_recv[n]
     piece[...] = whole_l * LEFT_SCALE
-    first_row = core * half + chip * rows_l
-    part = lax.rem(z, 8)
-    spot_l = lgrad.at[
-        pl.ds(pl.multiple_of(first_row + part // 4 * 8, 8), 8), pl.ds(pl.multiple_of(part % 4 * 128, 128), 128)
-    ]
-    own_l = pltpu.make_async_copy(piece, spot_l, own_sem.at[21])
-    own_l.start()
-    for d in (-4, 3, -3, 2, -2, 1, -1):
-        zz = z_peers[ZORDER.index(d)]
-        send(piece, spot_l, s_ss.at[11], s_rs.at[11], along_z(zz))
-    sum_r = right_local[pl.ds(pl.multiple_of(chip * 8, 8), 8), :]
+    z_gather[z] = piece[...]
+    for zz in z_peers:
+        send(piece, z_gather.at[z], s_ss.at[11], s_rs.at[11], along_z(zz))
+
+    z_part(3, 0, m1p, mixed_ref, MPARTS[2])
+    k1.wait()
+    k_half[...] = k_local[...] + k_core[...]
+    k2 = send(k_half, k_hi, s_ss.at[2], s_rs.at[2], across)
+
+    sum_r = right_local[number]
     bytes_of(right_xy, s_ss.at[6])
     bytes_of(right_xy, s_rs.at[6])
-    for j in range(NC - 1):
+    for j in range(2 * NC - 1):
         sum_r = sum_r + right_xy[j]
     right_half[...] = sum_r
     right_z[z] = sum_r
     for zz in z_peers:
         send(right_half, right_z.at[z], s_ss.at[7], s_rs.at[7], along_z(zz))
-    z_part(3, 0, m1p, mixed_ref, MPARTS[2])
 
     q_arrive(3, 1, mq1, m1)
     reorder(to_z, 1, m1, m1p)
@@ -370,10 +376,11 @@
     kernel_moved = move(k_total, k_home, 3, (dp, holder))
     z_part(3, 1, m1p, mixed_ref, LASTPARTS[1])
 
-    own_l.wait()
-    seven = z_recv.at[pl.ds(0, 7)]
-    bytes_of(seven, s_ss.at[11])
-    bytes_of(seven, s_rs.at[11])
+    bytes_of(z_tiles, s_ss.at[11])
+    bytes_of(z_tiles, s_rs.at[11])
+    for n in range(NZ):
+        own_rows[n // 4 * 4 : n // 4 * 4 + 4, n % 4 * 128 : n % 4 * 128 + 128] = z_gather[n]
+    lgrad[pl.ds(pl.multiple_of(core * half + chip * rows_l, rows_l), rows_l), :] = own_rows[...]
 
     def part_l(which, cc):
         return lgrad.at[pl.ds(pl.multiple_of(which * half + cc * rows_l, rows_l), rows_l)]
@@ -387,13 +394,10 @@
     whole_r = right_z[0]
     for n in range(1, NZ):
         whole_r = whole_r + right_z[n]
-    right_sum[...] = whole_r
-    rm = send(right_sum, right_mate, s_ss.at[4], s_rs.at[4], mate)
-    rm.wait()
-    right_piece[...] = (right_sum[...] + right_mate[...]) * RIGHT_SCALE
-    rgrad[pl.ds(pl.multiple_of(chip * 8, 8), 8), :] = right_piece[...]
-    for cc in chip_peers:
-        send(right_piece, block(rgrad, chip, 8), s_ss.at[10], s_rs.at[10], at_chip(cc))
+    right_piece[...] = whole_r * RIGHT_SCALE
+    right_all[number] = right_piece[...]
+    for there, n in plane_peers:
+        send(right_piece, right_all.at[number], s_ss.at[10], s_rs.at[10], there)
     for j, cc in enumerate(chip_peers):
         lx[j].wait_recv()
         send(part_l(core, cc), part_l(core, cc), x_ss.at[1], s_rs.at[12], mate)
@@ -405,6 +409,8 @@
     kernel_moved()
     bytes_of(right_xy, s_ss.at[10])
     bytes_of(right_xy, s_rs.at[10])
+    for n in range(2 * NC):
+        rgrad[4 * n : 4 * n + 4, :] = right_all[n]
     saves = [
         pltpu.make_async_copy(src, dst, own_sem.at[22 + n])
         for n, (src, dst) in enumerate([(k_home, kgrad_ref), (rgrad, rgrad_ref)])
@@ -449,7 +455,7 @@
     hbm = pl.BlockSpec(memory_space=pl.ANY)
     plane = pltpu.VMEM((S2, D), BF16)
     square = pltpu.VMEM((S2, S2), BF16)
-    tile, four = pltpu.VMEM((8, S1), F32), pltpu.VMEM((4, S1), F32)
+    four = pltpu.VMEM((4, S1), F32)
     half = S2 // 2
     dma = pltpu.SemaphoreType.DMA
     results = (
@@ -466,7 +472,7 @@
         in_specs=[hbm] * 5,
         out_specs=(hbm,) * 5,
         scratch_shapes=[
-            plane, square, pltpu.VMEM((S1, S1), BF16),
+            plane, plane, square, pltpu.VMEM((S1, S1), BF16),
             *[plane] * 12,
             pltpu.VMEM((S2, D), F32),
             *[plane] * 4,
@@ -474,13 +480,15 @@
             four, pltpu.VMEM((S2, S1), F32), pltpu.VMEM((S2, S1), F32),
             *[pltpu.VMEM((half, S2), F32)] * 3,
             pltpu.VMEM((NC - 1, half // NC, S2), F32),
-            pltpu.VMEM((8, 8, S1), F32), pltpu.VMEM((NZ, 8, S1), F32), tile,
-            pltpu.VMEM((S2, S2), F32), pltpu.VMEM((S2, S2), F32), pltpu.VMEM((S1, S1), F32),
-            pltpu.VMEM((NC - 1, 8, S1), F32), tile, tile, tile, pltpu.VMEM((NZ, 8, S1), F32), tile,
+            pltpu.VMEM((NZ, 4, S1), F32), pltpu.VMEM((NZ, 4, S1), F32), four, pltpu.VMEM((NZ, 4, S1), F32),
+            pltpu.VMEM((half // NC, S2), F32),
+            pltpu.VMEM((S2, S2), F32), pltpu.VMEM((S2, S2), F32), pltpu.VMEM((2 * NC, 4, S1), F32),
+            pltpu.VMEM((2 * NC - 1, 4, S1), F32), four, pltpu.VMEM((NZ, 4, S1), F32), four,
+            pltpu.VMEM((2 * NC, 4, S1), F32),
             pltpu.VMEM((S1, S1), F32),
             *[four] * 6,
-            dma((3,)), dma((25,)), dma((8,)), dma((8,)), dma((8,)), dma((8,)),
-            dma((13,)), dma((13,)), dma((2,)), dma((NC - 1,)),
+            dma((4,)), dma((25,)), dma((8,)), dma((8,)), dma((8,)), dma((8,)),
+            dma((14,)), dma((14,)), dma((2,)), dma((NC - 1,)),
         ],
         compiler_params=pltpu.CompilerParams(
             collective_id=0, has_side_effects=True, vmem_limit_bytes=VMEM_LIMIT

time: 164 us -> 165 us (level)
  no operation moved by 1% of the time
where the time goes in v4:
time: 165 us; the launch traced here: 164 us
  Pallas kernels  164 us (99%)
    pallas_call x1, Pallas kernels, on_device(): pl.pallas_call(kernel, name='monarch', out_shape=results, in_specs=[hbm]...  161 us

profile of v4, /device:TPU:1, one launch (start us, length us, event | category | flops | bytes accessed | tf_op | source)
XLA Modules:
  0.0 164.5 jit_solution(4337219098214751214)
XLA Ops:
  0.6 161.1 %monarch.1 = (bf16[512,768]{1,0:T(8,128)(2,1)}, bf16[512,768]{1,0:T(8,128)(2,1)}, f32[512,512]{1,0:T(8,128)}, f32[128,128]{1,0:T(8,128)}, f32[4,128]{1,0:T(4,128)}) custom-call(bf16[512,768]{1,0:T(8,128)(2,1)} %bitcast.6, bf16[512,512]{1,0:T(8,128)(2,1)} %left_hbm.1, bf16[128,128]{1,0:T(8,128)(2,1)} %right_hbm.1, f32[4,128]{1,0:T(4,128)} %bitcast.8, ...), custom_call_target="tpu_custom_call" | custom-call | tf_op jit(solution)/shard_map/monarch/pallas_call | solution.py:468
  161.7 2.8 %keep.1 = (bf16[512,768]{1,0:T(8,128)(2,1)}, bf16[512,768]{1,0:T(8,128)(2,1)}, f32[512,512]{1,0:T(8,128)}, f32[128,128]{1,0:T(8,128)}, f32[4,128]{1,0:T(4,128)}) custom-call(bf16[512,768]{1,0:T(8,128)(2,1)} %get-tuple-element.15.refs_0_, bf16[512,768]{1,0:T(8,128)(2,1)} %get-tuple-element.16.refs_1_, f32[512,512]{1,0:T(8,128)} %get-tuple-element.17.refs_2_, ...), custom_call_target="tpu_custom_call" | custom-call | tf_op jit(solution)/shard_map/keep/pallas_call | solution.py:497
